TPU v7x, 32 devices: a whole 2x2x4 slice. The times are simulated.
32 devices in a mesh: groups: 2 (over y), dp: 4 (over z), mp: 4 (over x, core).
Axes of the slice: x: 2, y: 2, z: 4, core: 2. Of those that a mesh axis runs over, the one named last changes fastest.
Arguments:
- activations: bfloat16 [1024, 5120], P(('groups', 'dp')), parts along dimension 0, may hold values from -6 to 6
- gradients: bfloat16 [1024, 12800], P(('groups', 'dp')), parts along dimension 0, may hold values from -6 to 6
- input_basis: bfloat16 [5120, 2560], P(None, 'mp'), may hold values from -0.078125 to 0.078125
- output_basis: bfloat16 [12800, 12800], P('dp', 'mp'), may hold values from -0.0546875 to 0.0546875
- lengths: int32 [32], P('groups'), parts along dimension 0, may hold values from 1 to 32, as said below
Outputs:
- corrected_eigenvalues: float32 [5120, 12800], P(('groups', 'dp'), 'mp'), parts along dimension 0
There are 2 independent parts, one for each index of `groups`. A program takes and returns all parts, laid end to end along the dimension named above; an argument that names none is the same for every part. Nothing has to cross between parts.
Inputs may be any that keep to these rules, and one draw needn't show every extreme that they name: `lengths`: at least one sequence has exactly 32 tokens.
All inputs are finite; a program needn't handle non-finite values.
Results may differ from a plain program's by a relative error of at most 0.012.
Values may be sent and summed in bfloat16 or wider, within the bound.
No kernel may reach another device: no remote copies, remote signals or barrier semaphores. Data moves between devices by JAX's collectives and lax.ppermute only.
A program may use at most 320 MiB of HBM per device.

v0:
```python
import functools

import jax
import jax.numpy as jnp
from jax import lax
from jax.experimental import pallas as pl
from jax.experimental.pallas import tpu as pltpu
from jax.sharding import PartitionSpec as P

TILE = 256
WINDOW = 128
ALIGN = 16
AHEAD = 4
STARTED = 1
EDGES = (0, 3, 7, 10, 13)
FEW_EDGES = (0, 6, 13)
MIB = 1024 * 1024


def column_chunks(width, marks):
    tiles = -(-width // TILE)
    edges = [tiles * c // marks[-1] for c in marks]
    return [
        (lo * TILE, min(hi * TILE, width) - lo * TILE)
        for lo, hi in zip(edges[:-1], edges[1:])
        if lo < hi
    ]


def compact_kernel(pieces, place_ref, *refs):
    sources, out, buf, sems = refs[: len(pieces)], refs[-3], refs[-2], refs[-1]
    copies = []
    row = 0
    for j, size in enumerate(pieces):
        copies.append(pltpu.make_async_copy(sources[j], buf.at[pl.ds(row, size)], sems.at[j]))
        copies[-1].start()
        row += size
    place = lax.broadcasted_iota(jnp.int32, (out.shape[0], row), 0)
    selector = jnp.where(place == place_ref[...], 1.0, 0.0).astype(jnp.bfloat16)
    for copy in copies:
        copy.wait()
    width = out.shape[1]
    step = 640 if width % 640 == 0 else width
    for lo in range(0, width, step):
        out[:, lo : lo + step] = jnp.dot(
            selector, buf[:, lo : lo + step], preferred_element_type=jnp.float32
        ).astype(out.dtype)


def compact(pieces, places, rows):
    sizes = tuple(p.shape[0] for p in pieces)
    width = pieces[0].shape[1]
    return pl.pallas_call(
        functools.partial(compact_kernel, sizes),
        in_specs=[pl.BlockSpec(memory_space=pltpu.VMEM)]
        + [pl.BlockSpec(memory_space=pl.ANY)] * len(pieces),
        out_specs=pl.BlockSpec(memory_space=pltpu.VMEM),
        scratch_shapes=[
            pltpu.VMEM((sum(sizes), width), jnp.bfloat16),
            pltpu.SemaphoreType.DMA((len(pieces),)),
        ],
        out_shape=jax.ShapeDtypeStruct((rows, width), jnp.bfloat16),
        compiler_params=pltpu.CompilerParams(
            vmem_limit_bytes=2 * width * (sum(sizes) + rows) + 8 * rows * sum(sizes) + 6 * MIB
        ),
        name="compact_rows",
    )(places[None, :], *pieces)


def rotate_kernel(rows_ref, basis_ref, out_ref):
    out_ref[...] = jnp.dot(
        rows_ref[...], basis_ref[...], preferred_element_type=jnp.float32
    ).astype(out_ref.dtype)


def rotate(rows, basis, first, size):
    depth = basis.shape[0]
    begin = first // TILE
    return pl.pallas_call(
        rotate_kernel,
        grid=(-(-size // TILE),),
        in_specs=[
            pl.BlockSpec(rows.shape, lambda j: (0, 0)),
            pl.BlockSpec((depth, TILE), lambda j: (0, begin + j)),
        ],
        out_specs=pl.BlockSpec((rows.shape[0], TILE), lambda j: (0, j)),
        out_shape=jax.ShapeDtypeStruct((rows.shape[0], size), jnp.bfloat16),
        compiler_params=pltpu.CompilerParams(
            vmem_limit_bytes=4 * (rows.size + depth * TILE) + 4 * rows.shape[0] * TILE + 6 * MIB
        ),
        cost_estimate=pl.CostEstimate(flops=1, bytes_accessed=1, transcendentals=0),
        name="rotate_chunk",
    )(rows, basis)


def squares_kernel(seqs, scale, window_starts, at_ref, gt_ref, *refs):
    out_ref = refs[-1]
    for n in range(seqs):
        start = pl.multiple_of(window_starts[n], ALIGN)
        summed = jnp.dot(
            at_ref[:, n * WINDOW : (n + 1) * WINDOW],
            gt_ref[pl.ds(start, WINDOW), :],
            preferred_element_type=jnp.float32,
        )
        squared = summed * summed
        if n == 0:
            out_ref[...] = squared
        elif n < seqs - 1:
            out_ref[...] += squared
        else:
            out_ref[...] = (out_ref[...] + squared) * scale


def squares(window_starts, at_windows, gt_chunk, scale, first, total_width, previous):
    seqs = window_starts.shape[0]
    directions = at_windows.shape[0]
    rows, size = gt_chunk.shape
    begin = first // TILE
    in_specs = [
        pl.BlockSpec(at_windows.shape, lambda j, ws: (0, 0)),
        pl.BlockSpec((rows, TILE), lambda j, ws: (0, j)),
    ]
    operands = [window_starts, at_windows, gt_chunk]
    aliases = {}
    if previous is not None:
        in_specs.append(pl.BlockSpec(memory_space=pl.ANY))
        operands.append(previous)
        aliases = {3: 0}
    return pl.pallas_call(
        functools.partial(squares_kernel, seqs, scale),
        grid_spec=pltpu.PrefetchScalarGridSpec(
            num_scalar_prefetch=1,
            grid=(-(-size // TILE),),
            in_specs=in_specs,
            out_specs=pl.BlockSpec((directions, TILE), lambda j, ws: (0, begin + j)),
        ),
        out_shape=jax.ShapeDtypeStruct((directions, total_width), jnp.float32),
        input_output_aliases=aliases,
        compiler_params=pltpu.CompilerParams(
            vmem_limit_bytes=4 * (at_windows.size + rows * TILE) + 16 * directions * TILE + 6 * MIB
        ),
        cost_estimate=pl.CostEstimate(flops=1, bytes_accessed=1, transcendentals=0),
        name="sum_squares",
    )(*operands)


def exchange_gradients(gradients, shards, parts):
    d, m = lax.axis_index("dp"), lax.axis_index("mp")
    rows, hidden = gradients.shape
    width = hidden // shards
    if shards == 4 and parts == 4:
        share = rows // parts
        mine = lax.dynamic_slice_in_dim(gradients, m * share, share, 0)
        own = lax.dynamic_slice_in_dim(gradients, d * width, width, 1)
        pieces, flips, steps = [own], [], []
        far, sent = [], []
        for k in (2, 1, 3):
            block = lax.dynamic_slice_in_dim(mine, lax.rem(d + k, shards) * width, width, 1)
            sent.append(block)
            far.append(lax.ppermute(block, "dp", [(e, (e + k) % shards) for e in range(shards)]))
        for k, received in zip((2, 1, 3), far):
            crossed = lax.ppermute(received, "mp", [(p, p ^ 2) for p in range(parts)])
            pieces += [received, crossed]
            for piece in (received, crossed):
                pieces.append(lax.ppermute(piece, "mp", [(p, p ^ 1) for p in range(parts)]))
            flips += [0, 2, 1, 3]
            steps += [k] * parts
        row = jnp.arange(rows * shards, dtype=jnp.int32)
        group = jnp.maximum(row - rows, 0) // share
        flip = sum(jnp.where(group == g, f, 0) for g, f in enumerate(flips))
        step = sum(jnp.where(group == g, k, 0) for g, k in enumerate(steps))
        near = row < rows
        from_shard = jnp.where(near, d, lax.rem(d + shards - step, shards))
        from_row = jnp.where(near, row, (m ^ flip) * share + row % share)
        return pieces, from_shard, from_row, sent, pieces[10:11]
    exchanged = lax.all_to_all(gradients, "dp", split_axis=1, concat_axis=0, tiled=True)
    row = jnp.arange(rows * shards, dtype=jnp.int32)
    return [exchanged], row // rows, row % rows, [], []


def stack_kernel(*refs):
    out, row = refs[-1], 0
    for ref in refs[:-1]:
        out[row : row + ref.shape[0], :] = ref[...]
        row += ref.shape[0]


def stack(pieces):
    shape = (sum(p.shape[0] for p in pieces), pieces[0].shape[1])
    return pl.pallas_call(
        stack_kernel,
        in_specs=[pl.BlockSpec(memory_space=pltpu.VMEM)] * len(pieces),
        out_specs=pl.BlockSpec(memory_space=pltpu.VMEM),
        out_shape=jax.ShapeDtypeStruct(shape, pieces[0].dtype),
        compiler_params=pltpu.CompilerParams(vmem_limit_bytes=8 * MIB),
        name="stack_rows",
    )(*pieces)


def at(e, p, parts):
    return e * parts + p


def collect_inputs(rotated_in, shards, parts):
    if shards != 4 or parts != 4:
        full = lax.all_gather(rotated_in, "mp", axis=1, tiled=True)
        return lax.all_to_all(full, "dp", split_axis=1, concat_axis=0, tiled=True)
    gathered = [rotated_in]
    for k in range(1, shards):
        pairs = [(at((p + k) % shards, p, parts), at(p, p, parts)) for p in range(parts)]
        gathered.append(lax.ppermute(rotated_in, ("dp", "mp"), pairs))
    return stack(gathered)


def spread_inputs(held, shards, parts):
    if shards != 4 or parts != 4:
        return held, jnp.arange(shards, dtype=jnp.int32)
    d, m = lax.axis_index("dp"), lax.axis_index("mp")
    axes = ("dp", "mp")
    pairs = [(at(p, p, parts), at(p, p ^ 2, parts)) for p in range(parts)]
    held = jnp.where(m == d, held, lax.ppermute(held, axes, pairs))
    pairs = [(at(p, p ^ q, parts), at(p, p ^ q ^ 1, parts)) for p in range(parts) for q in (0, 2)]
    swapped = lax.ppermute(held, axes, pairs)
    held = jnp.where((m == d) | (m == (d ^ 2)), held, swapped)
    return held, lax.rem(d + jnp.arange(shards, dtype=jnp.int32), shards)


def add_rounded(a, b):
    return (a.astype(jnp.float32) + b.astype(jnp.float32)).astype(jnp.bfloat16)


def after(x, *others):
    others = [o for o in others if o is not None]
    return lax.optimization_barrier((x, *others))[0] if others else x


def chunk_sums(rows, basis, chunks, shards, started):
    if shards != 4:
        parts = started + [rotate(rows, basis, *chunk) for chunk in chunks[len(started) :]]
        return [lax.psum(part, "dp") for part in parts]
    d = lax.axis_index("dp")
    middle = (d == 1) | (d == 2)
    count = len(chunks)
    parts, inward, pairs, across, sums, outward, done = ({} for _ in range(7))

    def begin(c):
        if c < count:
            if c < len(started):
                part = started[c]
            else:
                part = rotate(after(rows, parts.get(c - 1)), basis, *chunks[c])
            parts[c] = after(part, sums.get(c - AHEAD))
            inward[c] = lax.ppermute(parts[c], "dp", [(0, 1), (3, 2)])

    for c in range(AHEAD):
        begin(c)
    for s in range(count + 2):
        if s < count:
            pairs[s] = add_rounded(parts[s], after(inward[s], sums.get(s - 2), done.get(s - 3)))
            across[s] = lax.ppermute(pairs[s], "dp", [(1, 2), (2, 1)])
        if 1 <= s <= count:
            sums[s - 1] = add_rounded(pairs[s - 1], after(across[s - 1], pairs.get(s)))
            outward[s - 1] = lax.ppermute(sums[s - 1], "dp", [(1, 0), (2, 3)])
            begin(s - 1 + AHEAD)
        if s >= 2:
            got = after(outward[s - 2], sums.get(s - 1))
            done[s - 2] = jnp.where(middle, sums[s - 2], got)
    return [after(done[c], sums[min(c + 3, count - 1)]) for c in range(count)]


def rotate_and_square(
    shards, parts, bucket, places, tokens, seq_starts, seq_ends, output_basis, held, *pieces
):
    seqs = seq_starts.shape[0]
    rows = places.shape[0]
    shard_rows = rows // shards
    compacted = compact(pieces, places, bucket)
    width = output_basis.shape[1]
    chunks = column_chunks(width, EDGES if bucket < rows else FEW_EDGES)
    started = []
    for chunk in chunks[:STARTED]:
        started.append(rotate(after(compacted, *started[-1:]), output_basis, *chunk))
    held = after(held, *started[-1:])
    held, order = spread_inputs(collect_inputs(held, shards, parts), shards, parts)

    window_starts = jnp.minimum(seq_starts // ALIGN * ALIGN, bucket - WINDOW)
    place = window_starts[:, None] + jnp.arange(WINDOW, dtype=jnp.int32)[None, :]
    inside = (place >= seq_starts[:, None]) & (place < seq_ends[:, None])
    token = jnp.where(inside, place + tokens[:, None], -1).reshape(-1)
    held_token = (
        order[:, None] * shard_rows + jnp.arange(shard_rows, dtype=jnp.int32)[None, :]
    ).reshape(-1)
    selector = (held_token[:, None] == token[None, :]).astype(jnp.bfloat16)
    at_windows = lax.dot_general(
        held, selector, (((0,), (0,)), ((), ())), preferred_element_type=jnp.float32
    ).astype(jnp.bfloat16)

    sums = chunk_sums(compacted, output_basis, chunks, shards, started)
    result = None
    for (first, _), gt_chunk in zip(chunks, sums):
        result = squares(window_starts, at_windows, gt_chunk, 1.0 / rows, first, width, result)
    return result


def per_device(activations, gradients, input_basis, output_basis, lengths):
    groups, shards, parts = (lax.axis_size(name) for name in ("groups", "dp", "mp"))
    shard_rows = activations.shape[0]
    rows = shard_rows * shards
    seqs = lengths.shape[0]
    per_shard = seqs // shards

    pieces, from_shard, from_row, sent, crossed = exchange_gradients(gradients, shards, parts)
    rotated_in = jnp.dot(
        after(activations, *sent), input_basis, preferred_element_type=jnp.float32
    ).astype(jnp.bfloat16)

    seq_ends = jnp.cumsum(lengths, dtype=jnp.int32)
    seq_starts = seq_ends - lengths
    shard_ends = seq_ends[per_shard - 1 :: per_shard]
    shard_starts = seq_starts[::per_shard]
    tokens = (
        jnp.arange(shards, dtype=jnp.int32)[:, None] * shard_rows
        - shard_starts[:, None]
        + jnp.zeros((1, per_shard), jnp.int32)
    ).reshape(-1)
    at_shard = from_shard[:, None] == jnp.arange(shards, dtype=jnp.int32)[None, :]
    places = from_row + jnp.sum(jnp.where(at_shard, shard_starts[None, :], 0), axis=1)
    limits = jnp.sum(jnp.where(at_shard, shard_ends[None, :], 0), axis=1)
    places = jnp.where(places < limits, places, -1)

    held = rotated_in
    operands = lax.optimization_barrier((places, tokens, seq_starts, seq_ends, output_basis, held, *pieces))
    if shards != 4 or parts != 4:
        return rotate_and_square(shards, parts, rows, *operands)
    total = after(seq_ends[-1:], rotated_in)
    if groups == 2:
        total = jnp.maximum(total, lax.ppermute(total, "groups", [(0, 1), (1, 0)]))
    elif groups > 2:
        total = lax.pmax(total, "groups")
    buckets = [rows // 16 * k for k in (11, 16)]
    index = sum((total[0] > size).astype(jnp.int32) for size in buckets[:-1])
    branches = [functools.partial(rotate_and_square, shards, parts, size) for size in buckets]
    return lax.switch(index, branches, *operands)


def solution(mesh):
    placed = (
        P(("groups", "dp"), None),
        P(("groups", "dp"), None),
        P(None, "mp"),
        P("dp", "mp"),
        P("groups"),
    )
    return jax.shard_map(
        per_device, mesh=mesh, in_specs=placed, out_specs=P(("groups", "dp"), "mp"), check_vma=False
    )
```

profile of v0, /device:TPU:13, one launch (start us, length us, event | category | flops | bytes accessed | tf_op | source)
XLA Modules:
  0.0 154.3 jit_solution(12135186572748048670)
XLA Ops:
  0.0 1.5 fusion.51
  1.8 1.3 collective-permute-start.33
  3.0 4.1 %collective-permute-start.29 = (bf16[32,3200]{1,0:T(8,128)(2,1)S(1)}, bf16[32,3200]{1,0:T(8,128)(2,1)S(1)}, u32[]{:S(2)}, u32[]{:S(2)}) collective-permute-start(bf16[32,3200]{1,0:T(8,128)(2,1)S(1)} %get-tuple-element.191), channel_id=1, source_target_pairs={{0,8},{4,12},{8,0},{12,4},{1,9},{5,13},{9,1},{13,5},{2,10},{6,14},... | collective-permute-start | bytes 614408 | tf_op jit(solution)/shard_map/ppermute | solution.py:160
  8.4 4.1 %convolution_convert_fusion = bf16[128,640]{1,0:T(8,128)(2,1)S(1)} fusion(bf16[128,5120]{1,0:T(8,128)(2,1)S(1)} %copy-done, bf16[5120,640]{1,0:T(8,128)(2,1)} %param.9), kind=kOutput, calls=%fused_computation.64 | convolution fusion | flops 838942720 | bytes 8028160 | tf_op jit(solution)/shard_map/dot_general | solution.py:313
  13.1 1.2 constant_dynamic-slice_fusion
  14.5 1.8 %collective-permute-start.39 = (bf16[32,3200]{1,0:T(8,128)(2,1)S(1)}, bf16[32,3200]{1,0:T(8,128)(2,1)S(1)}, u32[]{:S(2)}, u32[]{:S(2)}) collective-permute-start(bf16[32,3200]{1,0:T(8,128)(2,1)S(1)} %collective-permute-done.37), channel_id=1, source_target_pairs={{0,1},{1,0},{2,3},{3,2},{4,5},{5,4},{6,7},{7,6},{8,9},{9,8},{10,11... | collective-permute-start | bytes 614408 | tf_op jit(solution)/shard_map/ppermute | solution.py:165
  16.3 3.9 %collective-permute-start.38 = (bf16[32,3200]{1,0:T(8,128)(2,1)S(1)}, bf16[32,3200]{1,0:T(8,128)(2,1)S(1)}, u32[]{:S(2)}, u32[]{:S(2)}) collective-permute-start(bf16[32,3200]{1,0:T(8,128)(2,1)S(1)} %collective-permute-done.37), channel_id=1, source_target_pairs={{0,2},{1,3},{2,0},{3,1},{4,6},{5,7},{6,4},{7,5},{8,10},{9,11},{10,... | collective-permute-start | bytes 614408 | tf_op jit(solution)/shard_map/ppermute | solution.py:162
  20.2 1.5 collective-permute-start.30
  21.8 1.4 collective-permute-start.35
  23.3 2.3 %collective-permute-done.38 = bf16[32,3200]{1,0:T(8,128)(2,1)S(1)} collective-permute-done((bf16[32,3200]{1,0:T(8,128)(2,1)S(1)}, bf16[32,3200]{1,0:T(8,128)(2,1)S(1)}, u32[]{:S(2)}, u32[]{:S(2)}) %collective-permute-start.38) | collective-permute-done | bytes 204832 | tf_op jit(solution)/shard_map/ppermute | solution.py:162
  26.4 3.6 %collective-permute-done.34 = bf16[32,3200]{1,0:T(8,128)(2,1)S(1)} collective-permute-done((bf16[32,3200]{1,0:T(8,128)(2,1)S(1)}, bf16[32,3200]{1,0:T(8,128)(2,1)S(1)}, u32[]{:S(2)}, u32[]{:S(2)}) %collective-permute-start.34) | collective-permute-done | bytes 204832 | tf_op jit(solution)/shard_map/ppermute | solution.py:162
  30.8 3.6 %collective-permute-done.30 = bf16[32,3200]{1,0:T(8,128)(2,1)S(1)} collective-permute-done((bf16[32,3200]{1,0:T(8,128)(2,1)S(1)}, bf16[32,3200]{1,0:T(8,128)(2,1)S(1)}, u32[]{:S(2)}, u32[]{:S(2)}) %collective-permute-start.30) | collective-permute-done | bytes 204832 | tf_op jit(solution)/shard_map/ppermute | solution.py:162
  36.4 116.6 %conditional.1 = (f32[640,3200]{1,0:T(8,128)}) conditional(s32[]{:T(128)} %bitcast.8, (s32[16]{0:T(128)S(1)}, s32[512]{0:T(512)S(1)}, bf16[128,3200]{1,0:T(8,128)(2,1)S(1)}, bf16[32,3200]{1,0:T(8,128)(2,1)S(1)}, bf16[32,3200]{1,0:T(8,128)(2,1)S(1)}, /*index=5*/bf16[32,3200]{1,0:T(8,128)(2,1)S(1)}, bf16[32,3200]{1,0:T(8,128)(2,1)S(1)}, ...), branch_computations={%region_3.4_spmd, %region_4.5_spmd} | conditional | flops 1359950592 | bytes 166810688 | solution.py:343
  36.4 5.6 %compact_rows.2.rows_ref = bf16[352,3200]{1,0:T(8,128)(2,1)S(1)} custom-call(s32[1,512]{1,0:T(1,128)S(1)} %bitcast.15, bf16[128,3200]{1,0:T(8,128)(2,1)S(1)} %get-tuple-element.87.refs_0_, bf16[32,3200]{1,0:T(8,128)(2,1)S(1)} %get-tuple-element.88.refs_1_, bf16[32,3200]{1,0:T(8,128)(2,1)S(1)} %get-tuple-element.89.refs_2_, ...), custom_call_target="tpu_custom_call" | custom-call | tf_op jit(solution)/shard_map/cond/branch_0_fun/compact_rows/pallas_call | solution.py:53
  42.0 5.0 %rotate_chunk.6 = bf16[352,768]{1,0:T(8,128)(2,1)S(1)} custom-call(bf16[352,3200]{1,0:T(8,128)(2,1)S(1)} %compact_rows.2.rows_ref, bf16[3200,3200]{1,0:T(8,128)(2,1)} %get-tuple-element.100.basis_ref), custom_call_target="tpu_custom_call" | custom-call | flops 1 | bytes 1 | tf_op jit(solution)/shard_map/cond/branch_0_fun/rotate_chunk/pallas_call | solution.py:79
  47.0 1.6 %collective-permute-start.2 = (bf16[128,640]{1,0:T(8,128)(2,1)S(1)}, bf16[128,640]{1,0:T(8,128)(2,1)S(1)}, u32[]{:S(2)}, u32[]{:S(2)}) collective-permute-start(bf16[128,640]{1,0:T(8,128)(2,1)S(1)} %get-tuple-element.101.refs_0_), channel_id=1, source_target_pairs={{12,0},{1,5},{6,10},{11,15},{28,16},{17,21},{22,26},{27,31}} | collective-permute-start | bytes 491528 | tf_op jit(solution)/shard_map/cond/branch_0_fun/ppermute | solution.py:211
  48.6 1.6 %collective-permute-start.1 = (bf16[128,640]{1,0:T(8,128)(2,1)S(1)}, bf16[128,640]{1,0:T(8,128)(2,1)S(1)}, u32[]{:S(2)}, u32[]{:S(2)}) collective-permute-start(bf16[128,640]{1,0:T(8,128)(2,1)S(1)} %get-tuple-element.101.refs_0_), channel_id=1, source_target_pairs={{8,0},{13,5},{2,10},{7,15},{24,16},{29,21},{18,26},{23,31}} | collective-permute-start | bytes 491528 | tf_op jit(solution)/shard_map/cond/branch_0_fun/ppermute | solution.py:211
  50.1 1.3 collective-permute-start
  51.4 1.3 collective-permute-start.9
  52.8 3.8 %rotate_chunk.7 = bf16[352,1024]{1,0:T(8,128)(2,1)S(1)} custom-call(bf16[352,3200]{1,0:T(8,128)(2,1)S(1)} %compact_rows.2.rows_ref, bf16[3200,3200]{1,0:T(8,128)(2,1)S(1)} %copy-done.2), custom_call_target="tpu_custom_call" | custom-call | flops 1 | bytes 1 | tf_op jit(solution)/shard_map/cond/branch_0_fun/rotate_chunk/pallas_call | solution.py:79
  56.5 1.3 collective-permute-start.6
  57.9 2.8 %rotate_chunk.8 = bf16[352,768]{1,0:T(8,128)(2,1)S(1)} custom-call(bf16[352,3200]{1,0:T(8,128)(2,1)S(1)} %compact_rows.2.rows_ref, bf16[3200,3200]{1,0:T(8,128)(2,1)S(1)} %copy-done.2), custom_call_target="tpu_custom_call" | custom-call | flops 1 | bytes 1 | tf_op jit(solution)/shard_map/cond/branch_0_fun/rotate_chunk/pallas_call | solution.py:79
  60.7 3.0 %rotate_chunk.9 = bf16[352,640]{1,0:T(8,128)(2,1)S(1)} custom-call(bf16[352,3200]{1,0:T(8,128)(2,1)S(1)} %compact_rows.2.rows_ref, bf16[3200,3200]{1,0:T(8,128)(2,1)S(1)} %copy-done.2), custom_call_target="tpu_custom_call" | custom-call | flops 1 | bytes 1 | tf_op jit(solution)/shard_map/cond/branch_0_fun/rotate_chunk/pallas_call | solution.py:79
  63.7 1.3 collective-permute-start.8
  65.0 1.3 collective-permute-start.5
  67.3 2.9 %collective-permute-start.3 = (bf16[512,640]{1,0:T(8,128)(2,1)S(1)}, bf16[512,640]{1,0:T(8,128)(2,1)}, u32[]{:S(2)}, u32[]{:S(2)}) collective-permute-start(bf16[512,640]{1,0:T(8,128)(2,1)S(1)} %stack_rows.2), channel_id=1, source_target_pairs={{0,2},{5,7},{10,8},{15,13},{16,18},{21,23},{26,24},{31,29}} | collective-permute-start | bytes 1966088 | tf_op jit(solution)/shard_map/cond/branch_0_fun/ppermute | solution.py:221
  70.3 1.2 add_convert_fusion.5
  71.5 2.6 %collective-permute-start.10 = (bf16[352,768]{1,0:T(8,128)(2,1)S(1)}, bf16[352,768]{1,0:T(8,128)(2,1)S(1)}, u32[]{:S(2)}, u32[]{:S(2)}) collective-permute-start(bf16[352,768]{1,0:T(8,128)(2,1)S(1)} %add_convert_fusion.5), channel_id=1, source_target_pairs={{4,8},{8,4},{5,9},{9,5},{6,10},{10,6},{7,11},{11,7},{20,24},{24,20... | collective-permute-start | bytes 1622024 | tf_op jit(solution)/shard_map/cond/branch_0_fun/ppermute | solution.py:260
  74.1 9.0 %collective-permute-done.6 = bf16[352,1024]{1,0:T(8,128)(2,1)} collective-permute-done((bf16[352,1024]{1,0:T(8,128)(2,1)S(1)}, bf16[352,1024]{1,0:T(8,128)(2,1)}, u32[]{:S(2)}, u32[]{:S(2)}) %collective-permute-start.6) | collective-permute-done | bytes 720928 | tf_op jit(solution)/shard_map/cond/branch_0_fun/ppermute | solution.py:253
  83.2 1.4 add_convert_fusion.1
  84.5 4.1 %collective-permute-start.7 = (bf16[352,1024]{1,0:T(8,128)(2,1)S(1)}, bf16[352,1024]{1,0:T(8,128)(2,1)S(1)}, u32[]{:S(2)}, u32[]{:S(2)}) collective-permute-start(bf16[352,1024]{1,0:T(8,128)(2,1)S(1)} %add_convert_fusion.1), channel_id=1, source_target_pairs={{4,8},{8,4},{5,9},{9,5},{6,10},{10,6},{7,11},{11,7},{20,24},{24,20... | collective-permute-start | bytes 2162696 | tf_op jit(solution)/shard_map/cond/branch_0_fun/ppermute | solution.py:260
  88.7 1.3 collective-permute-start.4
  90.2 1.3 collective-permute-start.11
  91.6 3.2 %collective-permute-done.8 = bf16[352,768]{1,0:T(8,128)(2,1)} collective-permute-done((bf16[352,768]{1,0:T(8,128)(2,1)S(1)}, bf16[352,768]{1,0:T(8,128)(2,1)}, u32[]{:S(2)}, u32[]{:S(2)}) %collective-permute-start.8) | collective-permute-done | bytes 540704 | tf_op jit(solution)/shard_map/cond/branch_0_fun/ppermute | solution.py:253
  95.9 4.1 %collective-permute-start.14 = (bf16[352,768]{1,0:T(8,128)(2,1)S(1)}, bf16[352,768]{1,0:T(8,128)(2,1)S(1)}, u32[]{:S(2)}, u32[]{:S(2)}) collective-permute-start(bf16[352,768]{1,0:T(8,128)(2,1)S(1)} %add_convert_fusion.3), channel_id=1, source_target_pairs={{4,8},{8,4},{5,9},{9,5},{6,10},{10,6},{7,11},{11,7},{20,24},{24,20... | collective-permute-start | bytes 1622024 | tf_op jit(solution)/shard_map/cond/branch_0_fun/ppermute | solution.py:260
  100.0 5.4 %collective-permute-done.7 = bf16[352,1024]{1,0:T(8,128)(2,1)S(1)} collective-permute-done((bf16[352,1024]{1,0:T(8,128)(2,1)S(1)}, bf16[352,1024]{1,0:T(8,128)(2,1)S(1)}, u32[]{:S(2)}, u32[]{:S(2)}) %collective-permute-start.7) | collective-permute-done | bytes 720928 | tf_op jit(solution)/shard_map/cond/branch_0_fun/ppermute | solution.py:260
  105.6 1.3 collective-permute-start.16
  108.2 3.5 %collective-permute-start.12 = (bf16[352,640]{1,0:T(8,128)(2,1)S(1)}, bf16[352,640]{1,0:T(8,128)(2,1)S(1)}, u32[]{:S(2)}, u32[]{:S(2)}) collective-permute-start(bf16[352,640]{1,0:T(8,128)(2,1)S(1)} %add_convert_fusion.7), channel_id=1, source_target_pairs={{4,8},{8,4},{5,9},{9,5},{6,10},{10,6},{7,11},{11,7},{20,24},{24,20... | collective-permute-start | bytes 1351688 | tf_op jit(solution)/shard_map/cond/branch_0_fun/ppermute | solution.py:260
  111.8 5.2 %collective-permute-done.14 = bf16[352,768]{1,0:T(8,128)(2,1)S(1)} collective-permute-done((bf16[352,768]{1,0:T(8,128)(2,1)S(1)}, bf16[352,768]{1,0:T(8,128)(2,1)S(1)}, u32[]{:S(2)}, u32[]{:S(2)}) %collective-permute-start.14) | collective-permute-done | bytes 540704 | tf_op jit(solution)/shard_map/cond/branch_0_fun/ppermute | solution.py:260
  117.1 1.3 collective-permute-start.15
  118.4 1.8 %fusion.2.at_ref = bf16[640,2048]{1,0:T(8,128)(2,1)S(1)} fusion(s32[2048]{0:T(1024)S(1)} %select_bitcast_fusion, s32[512]{0:T(512)S(1)} %add_bitcast_fusion, bf16[512,640]{1,0:T(8,128)(2,1)S(1)} %broadcast_select_fusion.1, bf16[512,640]{1,0:T(8,128)(2,1)S(1)} %collective-permute-done.4, pred[]{:T(512)S(6)} %or.8), kind=kOutput, calls=%fused_computation.2 | convolution fusion | flops 1344864256 | bytes 3942401 | tf_op jit(solution)/shard_map/cond/branch_0_fun/dot_general | solution.py:294
  120.2 4.5 %collective-permute-done.12 = bf16[352,640]{1,0:T(8,128)(2,1)S(1)} collective-permute-done((bf16[352,640]{1,0:T(8,128)(2,1)S(1)}, bf16[352,640]{1,0:T(8,128)(2,1)S(1)}, u32[]{:S(2)}, u32[]{:S(2)}) %collective-permute-start.12) | collective-permute-done | bytes 450592 | tf_op jit(solution)/shard_map/cond/branch_0_fun/ppermute | solution.py:260
  124.9 1.3 collective-permute-start.13
  126.2 6.2 %sum_squares.6.refs_0_ = f32[640,3200]{1,0:T(8,128)} custom-call(s32[16]{0:T(128)S(1)} %multiply_minimum_fusion.window_starts, bf16[640,2048]{1,0:T(8,128)(2,1)S(1)} %fusion.2.at_ref, bf16[352,768]{1,0:T(8,128)(2,1)S(1)} %broadcast_select_fusion.3.gt_ref), custom_call_target="tpu_custom_call" | custom-call | flops 1 | bytes 1 | tf_op jit(solution)/shard_map/cond/branch_0_fun/sum_squares/pallas_call | solution.py:129
  132.5 7.9 %sum_squares.7.refs_0_ = f32[640,3200]{1,0:T(8,128)} custom-call(s32[16]{0:T(128)S(1)} %multiply_minimum_fusion.window_starts, bf16[640,2048]{1,0:T(8,128)(2,1)S(1)} %fusion.2.at_ref, bf16[352,1024]{1,0:T(8,128)(2,1)S(1)} %broadcast_select_fusion.gt_ref, f32[640,3200]{1,0:T(8,128)} %sum_squares.6.refs_0_), custom_call_target="tpu_custom_call", output_to_operand_aliasing={{}: (3, {})} | custom-call | flops 1 | bytes 1 | tf_op jit(solution)/shard_map/cond/branch_0_fun/sum_squares/pallas_call | solution.py:129
  140.5 6.2 %sum_squares.8.refs_0_ = f32[640,3200]{1,0:T(8,128)} custom-call(s32[16]{0:T(128)S(1)} %multiply_minimum_fusion.window_starts, bf16[640,2048]{1,0:T(8,128)(2,1)S(1)} %fusion.2.at_ref, bf16[352,768]{1,0:T(8,128)(2,1)S(1)} %broadcast_select_fusion.2.gt_ref, f32[640,3200]{1,0:T(8,128)} %sum_squares.7.refs_0_), custom_call_target="tpu_custom_call", output_to_operand_aliasing={{}: (3, {})} | custom-call | flops 1 | bytes 1 | tf_op jit(solution)/shard_map/cond/branch_0_fun/sum_squares/pallas_call | solution.py:129
  146.8 6.2 %sum_squares.9 = f32[640,3200]{1,0:T(8,128)} custom-call(s32[16]{0:T(128)S(1)} %multiply_minimum_fusion.window_starts, bf16[640,2048]{1,0:T(8,128)(2,1)S(1)} %fusion.2.at_ref, bf16[352,640]{1,0:T(8,128)(2,1)S(1)} %broadcast_select_fusion.4.gt_ref, f32[640,3200]{1,0:T(8,128)} %sum_squares.8.refs_0_), custom_call_target="tpu_custom_call", output_to_operand_aliasing={{}: (3, {})} | custom-call | flops 1 | bytes 1 | tf_op jit(solution)/shard_map/cond/branch_0_fun/sum_squares/pallas_call | solution.py:129
  153.0 1.3 copy-done.1
  (67 shorter events, 9.2 us)
Async XLA Ops:
  0.0 8.4 %copy-start = (bf16[128,5120]{1,0:T(8,128)(2,1)S(1)}, bf16[128,5120]{1,0:T(8,128)(2,1)}, u32[]{:S(2)}) copy-start(bf16[128,5120]{1,0:T(8,128)(2,1)} %param.7) | copy-start | bytes 3932164
  1.5 13.0 %collective-permute-start.37 = (bf16[32,3200]{1,0:T(8,128)(2,1)S(1)}, bf16[32,3200]{1,0:T(8,128)(2,1)S(1)}, u32[]{:S(2)}, u32[]{:S(2)}) collective-permute-start(bf16[32,3200]{1,0:T(8,128)(2,1)S(1)} %get-tuple-element.189), channel_id=1, source_target_pairs={{0,12},{4,0},{8,4},{12,8},{1,13},{5,1},{9,5},{13,9},{2,14},{6,2},{... | collective-permute-start | bytes 614408 | tf_op jit(solution)/shard_map/ppermute | solution.py:160
  1.8 18.4 %collective-permute-start.33 = (bf16[32,3200]{1,0:T(8,128)(2,1)S(1)}, bf16[32,3200]{1,0:T(8,128)(2,1)S(1)}, u32[]{:S(2)}, u32[]{:S(2)}) collective-permute-start(bf16[32,3200]{1,0:T(8,128)(2,1)S(1)} %get-tuple-element.190), channel_id=1, source_target_pairs={{0,4},{4,8},{8,12},{12,0},{1,5},{5,9},{9,13},{13,1},{2,6},{6,10},{... | collective-permute-start | bytes 614408 | tf_op jit(solution)/shard_map/ppermute | solution.py:160
  3.0 17.2 %collective-permute-start.29 = (bf16[32,3200]{1,0:T(8,128)(2,1)S(1)}, bf16[32,3200]{1,0:T(8,128)(2,1)S(1)}, u32[]{:S(2)}, u32[]{:S(2)}) collective-permute-start(bf16[32,3200]{1,0:T(8,128)(2,1)S(1)} %get-tuple-element.191), channel_id=1, source_target_pairs={{0,8},{4,12},{8,0},{12,4},{1,9},{5,13},{9,1},{13,5},{2,10},{6,14},... | collective-permute-start | bytes 614408 | tf_op jit(solution)/shard_map/ppermute | solution.py:160
  8.4 4.5 %copy-start.9 = (s32[16]{0:T(128)S(1)}, s32[16]{0:T(128)}, u32[]{:S(2)}) copy-start(s32[16]{0:T(128)} %param.11) | copy-start | bytes 196
  12.5 9.3 %collective-permute-start.28 = (s32[1]{0:T(128)}, s32[1]{0:T(128)}, u32[]{:S(2)}, u32[]{:S(2)}) collective-permute-start(s32[1]{0:T(128)} %bitcast.7), channel_id=1, source_target_pairs={{0,16},{16,0},{1,17},{17,1},{2,18},{18,2},{3,19},{19,3},{4,20},{20... | collective-permute-start | bytes 20 | tf_op jit(solution)/shard_map/ppermute | solution.py:337
  14.5 8.7 %collective-permute-start.39 = (bf16[32,3200]{1,0:T(8,128)(2,1)S(1)}, bf16[32,3200]{1,0:T(8,128)(2,1)S(1)}, u32[]{:S(2)}, u32[]{:S(2)}) collective-permute-start(bf16[32,3200]{1,0:T(8,128)(2,1)S(1)} %collective-permute-done.37), channel_id=1, source_target_pairs={{0,1},{1,0},{2,3},{3,2},{4,5},{5,4},{6,7},{7,6},{8,9},{9,8},{10,11... | collective-permute-start | bytes 614408 | tf_op jit(solution)/shard_map/ppermute | solution.py:165
  16.3 9.3 %collective-permute-start.38 = (bf16[32,3200]{1,0:T(8,128)(2,1)S(1)}, bf16[32,3200]{1,0:T(8,128)(2,1)S(1)}, u32[]{:S(2)}, u32[]{:S(2)}) collective-permute-start(bf16[32,3200]{1,0:T(8,128)(2,1)S(1)} %collective-permute-done.37), channel_id=1, source_target_pairs={{0,2},{1,3},{2,0},{3,1},{4,6},{5,7},{6,4},{7,5},{8,10},{9,11},{10,... | collective-permute-start | bytes 614408 | tf_op jit(solution)/shard_map/ppermute | solution.py:162
  20.2 9.8 %collective-permute-start.34 = (bf16[32,3200]{1,0:T(8,128)(2,1)S(1)}, bf16[32,3200]{1,0:T(8,128)(2,1)S(1)}, u32[]{:S(2)}, u32[]{:S(2)}) collective-permute-start(bf16[32,3200]{1,0:T(8,128)(2,1)S(1)} %collective-permute-done.33), channel_id=1, source_target_pairs={{0,2},{1,3},{2,0},{3,1},{4,6},{5,7},{6,4},{7,5},{8,10},{9,11},{10,... | collective-permute-start | bytes 614408 | tf_op jit(solution)/shard_map/ppermute | solution.py:162
  20.2 14.2 %collective-permute-start.30 = (bf16[32,3200]{1,0:T(8,128)(2,1)S(1)}, bf16[32,3200]{1,0:T(8,128)(2,1)S(1)}, u32[]{:S(2)}, u32[]{:S(2)}) collective-permute-start(bf16[32,3200]{1,0:T(8,128)(2,1)S(1)} %collective-permute-done.29), channel_id=1, source_target_pairs={{0,2},{1,3},{2,0},{3,1},{4,6},{5,7},{6,4},{7,5},{8,10},{9,11},{10,... | collective-permute-start | bytes 614408 | tf_op jit(solution)/shard_map/ppermute | solution.py:162
  21.8 14.5 %collective-permute-start.35 = (bf16[32,3200]{1,0:T(8,128)(2,1)S(1)}, bf16[32,3200]{1,0:T(8,128)(2,1)S(1)}, u32[]{:S(2)}, u32[]{:S(2)}) collective-permute-start(bf16[32,3200]{1,0:T(8,128)(2,1)S(1)} %collective-permute-done.33), channel_id=1, source_target_pairs={{0,1},{1,0},{2,3},{3,2},{4,5},{5,4},{6,7},{7,6},{8,9},{9,8},{10,11... | collective-permute-start | bytes 614408 | tf_op jit(solution)/shard_map/ppermute | solution.py:165
  23.2 13.1 %collective-permute-start.31 = (bf16[32,3200]{1,0:T(8,128)(2,1)S(1)}, bf16[32,3200]{1,0:T(8,128)(2,1)S(1)}, u32[]{:S(2)}, u32[]{:S(2)}) collective-permute-start(bf16[32,3200]{1,0:T(8,128)(2,1)S(1)} %collective-permute-done.29), channel_id=1, source_target_pairs={{0,1},{1,0},{2,3},{3,2},{4,5},{5,4},{6,7},{7,6},{8,9},{9,8},{10,11... | collective-permute-start | bytes 614408 | tf_op jit(solution)/shard_map/ppermute | solution.py:165
  25.6 10.7 %collective-permute-start.40 = (bf16[32,3200]{1,0:T(8,128)(2,1)S(1)}, bf16[32,3200]{1,0:T(8,128)(2,1)}, u32[]{:S(2)}, u32[]{:S(2)}) collective-permute-start(bf16[32,3200]{1,0:T(8,128)(2,1)S(1)} %collective-permute-done.38), channel_id=1, source_target_pairs={{0,1},{1,0},{2,3},{3,2},{4,5},{5,4},{6,7},{7,6},{8,9},{9,8},{10,11... | collective-permute-start | bytes 614408 | tf_op jit(solution)/shard_map/ppermute | solution.py:165
  30.0 6.3 %collective-permute-start.36 = (bf16[32,3200]{1,0:T(8,128)(2,1)S(1)}, bf16[32,3200]{1,0:T(8,128)(2,1)S(1)}, u32[]{:S(2)}, u32[]{:S(2)}) collective-permute-start(bf16[32,3200]{1,0:T(8,128)(2,1)S(1)} %collective-permute-done.34), channel_id=1, source_target_pairs={{0,1},{1,0},{2,3},{3,2},{4,5},{5,4},{6,7},{7,6},{8,9},{9,8},{10,11... | collective-permute-start | bytes 614408 | tf_op jit(solution)/shard_map/ppermute | solution.py:165
  34.4 1.9 %collective-permute-start.32 = (bf16[32,3200]{1,0:T(8,128)(2,1)S(1)}, bf16[32,3200]{1,0:T(8,128)(2,1)S(1)}, u32[]{:S(2)}, u32[]{:S(2)}) collective-permute-start(bf16[32,3200]{1,0:T(8,128)(2,1)S(1)} %collective-permute-done.30), channel_id=1, source_target_pairs={{0,1},{1,0},{2,3},{3,2},{4,5},{5,4},{6,7},{7,6},{8,9},{9,8},{10,11... | collective-permute-start | bytes 614408 | tf_op jit(solution)/shard_map/ppermute | solution.py:165
  36.4 13.8 %copy-start.4 = (bf16[128,640]{1,0:T(8,128)(2,1)}, bf16[128,640]{1,0:T(8,128)(2,1)S(1)}, u32[]{:S(2)}) copy-start(bf16[128,640]{1,0:T(8,128)(2,1)S(1)} %get-tuple-element.101.refs_0_) | copy-start | bytes 491524 | tf_op jit(solution)/shard_map/cond
  42.0 10.7 %copy-start.2 = (bf16[3200,3200]{1,0:T(8,128)(2,1)S(1)}, bf16[3200,3200]{1,0:T(8,128)(2,1)}, u32[]{:S(2)}) copy-start(bf16[3200,3200]{1,0:T(8,128)(2,1)} %get-tuple-element.100.basis_ref) | copy-start | bytes 61440004 | tf_op jit(solution)/shard_map/cond
  47.0 16.7 %collective-permute-start.2 = (bf16[128,640]{1,0:T(8,128)(2,1)S(1)}, bf16[128,640]{1,0:T(8,128)(2,1)S(1)}, u32[]{:S(2)}, u32[]{:S(2)}) collective-permute-start(bf16[128,640]{1,0:T(8,128)(2,1)S(1)} %get-tuple-element.101.refs_0_), channel_id=1, source_target_pairs={{12,0},{1,5},{6,10},{11,15},{28,16},{17,21},{22,26},{27,31}} | collective-permute-start | bytes 491528 | tf_op jit(solution)/shard_map/cond/branch_0_fun/ppermute | solution.py:211
  48.6 16.5 %collective-permute-start.1 = (bf16[128,640]{1,0:T(8,128)(2,1)S(1)}, bf16[128,640]{1,0:T(8,128)(2,1)S(1)}, u32[]{:S(2)}, u32[]{:S(2)}) collective-permute-start(bf16[128,640]{1,0:T(8,128)(2,1)S(1)} %get-tuple-element.101.refs_0_), channel_id=1, source_target_pairs={{8,0},{13,5},{2,10},{7,15},{24,16},{29,21},{18,26},{23,31}} | collective-permute-start | bytes 491528 | tf_op jit(solution)/shard_map/cond/branch_0_fun/ppermute | solution.py:211
  50.1 16.2 %collective-permute-start = (bf16[128,640]{1,0:T(8,128)(2,1)S(1)}, bf16[128,640]{1,0:T(8,128)(2,1)S(1)}, u32[]{:S(2)}, u32[]{:S(2)}) collective-permute-start(bf16[128,640]{1,0:T(8,128)(2,1)S(1)} %get-tuple-element.101.refs_0_), channel_id=1, source_target_pairs={{4,0},{9,5},{14,10},{3,15},{20,16},{25,21},{30,26},{19,31}} | collective-permute-start | bytes 491528 | tf_op jit(solution)/shard_map/cond/branch_0_fun/ppermute | solution.py:211
  51.4 18.9 %collective-permute-start.9 = (bf16[352,768]{1,0:T(8,128)(2,1)S(1)}, bf16[352,768]{1,0:T(8,128)(2,1)}, u32[]{:S(2)}, u32[]{:S(2)}) collective-permute-start(bf16[352,768]{1,0:T(8,128)(2,1)S(1)} %rotate_chunk.6), channel_id=1, source_target_pairs={{0,4},{12,8},{1,5},{13,9},{2,6},{14,10},{3,7},{15,11},{16,20},{28,... | collective-permute-start | bytes 1622024 | tf_op jit(solution)/shard_map/cond/branch_0_fun/ppermute | solution.py:253
  56.5 26.6 %collective-permute-start.6 = (bf16[352,1024]{1,0:T(8,128)(2,1)S(1)}, bf16[352,1024]{1,0:T(8,128)(2,1)}, u32[]{:S(2)}, u32[]{:S(2)}) collective-permute-start(bf16[352,1024]{1,0:T(8,128)(2,1)S(1)} %rotate_chunk.7), channel_id=1, source_target_pairs={{0,4},{12,8},{1,5},{13,9},{2,6},{14,10},{3,7},{15,11},{16,20},{28,... | collective-permute-start | bytes 2162696 | tf_op jit(solution)/shard_map/cond/branch_0_fun/ppermute | solution.py:253
  63.7 31.0 %collective-permute-start.8 = (bf16[352,768]{1,0:T(8,128)(2,1)S(1)}, bf16[352,768]{1,0:T(8,128)(2,1)}, u32[]{:S(2)}, u32[]{:S(2)}) collective-permute-start(bf16[352,768]{1,0:T(8,128)(2,1)S(1)} %rotate_chunk.8), channel_id=1, source_target_pairs={{0,4},{12,8},{1,5},{13,9},{2,6},{14,10},{3,7},{15,11},{16,20},{28,... | collective-permute-start | bytes 1622024 | tf_op jit(solution)/shard_map/cond/branch_0_fun/ppermute | solution.py:253
  65.0 42.0 %collective-permute-start.5 = (bf16[352,640]{1,0:T(8,128)(2,1)S(1)}, bf16[352,640]{1,0:T(8,128)(2,1)}, u32[]{:S(2)}, u32[]{:S(2)}) collective-permute-start(bf16[352,640]{1,0:T(8,128)(2,1)S(1)} %rotate_chunk.9), channel_id=1, source_target_pairs={{0,4},{12,8},{1,5},{13,9},{2,6},{14,10},{3,7},{15,11},{16,20},{28,... | collective-permute-start | bytes 1351688 | tf_op jit(solution)/shard_map/cond/branch_0_fun/ppermute | solution.py:253
  67.3 21.3 %collective-permute-start.3 = (bf16[512,640]{1,0:T(8,128)(2,1)S(1)}, bf16[512,640]{1,0:T(8,128)(2,1)}, u32[]{:S(2)}, u32[]{:S(2)}) collective-permute-start(bf16[512,640]{1,0:T(8,128)(2,1)S(1)} %stack_rows.2), channel_id=1, source_target_pairs={{0,2},{5,7},{10,8},{15,13},{16,18},{21,23},{26,24},{31,29}} | collective-permute-start | bytes 1966088 | tf_op jit(solution)/shard_map/cond/branch_0_fun/ppermute | solution.py:221
  71.5 18.6 %collective-permute-start.10 = (bf16[352,768]{1,0:T(8,128)(2,1)S(1)}, bf16[352,768]{1,0:T(8,128)(2,1)S(1)}, u32[]{:S(2)}, u32[]{:S(2)}) collective-permute-start(bf16[352,768]{1,0:T(8,128)(2,1)S(1)} %add_convert_fusion.5), channel_id=1, source_target_pairs={{4,8},{8,4},{5,9},{9,5},{6,10},{10,6},{7,11},{11,7},{20,24},{24,20... | collective-permute-start | bytes 1622024 | tf_op jit(solution)/shard_map/cond/branch_0_fun/ppermute | solution.py:260
  84.5 20.8 %collective-permute-start.7 = (bf16[352,1024]{1,0:T(8,128)(2,1)S(1)}, bf16[352,1024]{1,0:T(8,128)(2,1)S(1)}, u32[]{:S(2)}, u32[]{:S(2)}) collective-permute-start(bf16[352,1024]{1,0:T(8,128)(2,1)S(1)} %add_convert_fusion.1), channel_id=1, source_target_pairs={{4,8},{8,4},{5,9},{9,5},{6,10},{10,6},{7,11},{11,7},{20,24},{24,20... | collective-permute-start | bytes 2162696 | tf_op jit(solution)/shard_map/cond/branch_0_fun/ppermute | solution.py:260
  88.7 29.7 %collective-permute-start.4 = (bf16[512,640]{1,0:T(8,128)(2,1)S(1)}, bf16[512,640]{1,0:T(8,128)(2,1)S(1)}, u32[]{:S(2)}, u32[]{:S(2)}) collective-permute-start(bf16[512,640]{1,0:T(8,128)(2,1)S(1)} %broadcast_select_fusion.1), channel_id=1, source_target_pairs={{0,1},{2,3},{5,4},{7,6},{10,11},{8,9},{15,14},{13,12},{16,17},{18,... | collective-permute-start | bytes 1966088 | tf_op jit(solution)/shard_map/cond/branch_0_fun/ppermute | solution.py:223
  90.2 16.7 %collective-permute-start.11 = (bf16[352,768]{1,0:T(8,128)(2,1)S(1)}, bf16[352,768]{1,0:T(8,128)(2,1)S(1)}, u32[]{:S(2)}, u32[]{:S(2)}) collective-permute-start(bf16[352,768]{1,0:T(8,128)(2,1)S(1)} %add_convert_fusion.4), channel_id=1, source_target_pairs={{4,0},{8,12},{5,1},{9,13},{6,2},{10,14},{7,3},{11,15},{20,16},{24,... | collective-permute-start | bytes 1622024 | tf_op jit(solution)/shard_map/cond/branch_0_fun/ppermute | solution.py:263
  95.9 21.0 %collective-permute-start.14 = (bf16[352,768]{1,0:T(8,128)(2,1)S(1)}, bf16[352,768]{1,0:T(8,128)(2,1)S(1)}, u32[]{:S(2)}, u32[]{:S(2)}) collective-permute-start(bf16[352,768]{1,0:T(8,128)(2,1)S(1)} %add_convert_fusion.3), channel_id=1, source_target_pairs={{4,8},{8,4},{5,9},{9,5},{6,10},{10,6},{7,11},{11,7},{20,24},{24,20... | collective-permute-start | bytes 1622024 | tf_op jit(solution)/shard_map/cond/branch_0_fun/ppermute | solution.py:260
  105.6 26.8 %collective-permute-start.16 = (bf16[352,1024]{1,0:T(8,128)(2,1)S(1)}, bf16[352,1024]{1,0:T(8,128)(2,1)S(1)}, u32[]{:S(2)}, u32[]{:S(2)}) collective-permute-start(bf16[352,1024]{1,0:T(8,128)(2,1)S(1)} %add_convert_fusion), channel_id=1, source_target_pairs={{4,0},{8,12},{5,1},{9,13},{6,2},{10,14},{7,3},{11,15},{20,16},{24,... | collective-permute-start | bytes 2162696 | tf_op jit(solution)/shard_map/cond/branch_0_fun/ppermute | solution.py:263
  108.2 16.5 %collective-permute-start.12 = (bf16[352,640]{1,0:T(8,128)(2,1)S(1)}, bf16[352,640]{1,0:T(8,128)(2,1)S(1)}, u32[]{:S(2)}, u32[]{:S(2)}) collective-permute-start(bf16[352,640]{1,0:T(8,128)(2,1)S(1)} %add_convert_fusion.7), channel_id=1, source_target_pairs={{4,8},{8,4},{5,9},{9,5},{6,10},{10,6},{7,11},{11,7},{20,24},{24,20... | collective-permute-start | bytes 1351688 | tf_op jit(solution)/shard_map/cond/branch_0_fun/ppermute | solution.py:260
  117.1 23.3 %collective-permute-start.15 = (bf16[352,768]{1,0:T(8,128)(2,1)S(1)}, bf16[352,768]{1,0:T(8,128)(2,1)S(1)}, u32[]{:S(2)}, u32[]{:S(2)}) collective-permute-start(bf16[352,768]{1,0:T(8,128)(2,1)S(1)} %add_convert_fusion.2), channel_id=1, source_target_pairs={{4,0},{8,12},{5,1},{9,13},{6,2},{10,14},{7,3},{11,15},{20,16},{24,... | collective-permute-start | bytes 1622024 | tf_op jit(solution)/shard_map/cond/branch_0_fun/ppermute | solution.py:263
  124.9 21.9 %collective-permute-start.13 = (bf16[352,640]{1,0:T(8,128)(2,1)S(1)}, bf16[352,640]{1,0:T(8,128)(2,1)S(1)}, u32[]{:S(2)}, u32[]{:S(2)}) collective-permute-start(bf16[352,640]{1,0:T(8,128)(2,1)S(1)} %add_convert_fusion.6), channel_id=1, source_target_pairs={{4,0},{8,12},{5,1},{9,13},{6,2},{10,14},{7,3},{11,15},{20,16},{24,... | collective-permute-start | bytes 1351688 | tf_op jit(solution)/shard_map/cond/branch_0_fun/ppermute | solution.py:263
  153.0 1.3 copy-start.1
where the time goes:
time: 155 us; the launch traced here: 154 us
  starting transfers between devices  50.1 us (32%)
  Pallas kernels  47.7 us (31%)
  waiting for transfers between devices  36.9 us (24%)
  other arithmetic  6.35 us (4%)
  matrix products  5.84 us (4%)
  local copies, waits for them, and re-layouts  5.65 us (4%)
    pallas_call x4, Pallas kernels, squares(): pl.pallas_call(functools.partial(squares_kernel, seqs, scale), grid_spec=...  26.6 us
    ppermute x4, waiting for transfers between devices, chunk_sums(): across[s] = lax.ppermute(pairs[s], 'dp', [(1, 2), (2, 1)])  15.1 us
    pallas_call x4, Pallas kernels, rotate(): pl.pallas_call(rotate_kernel, grid=(-(-size // TILE),), in_specs=[pl.Bloc...  14.5 us
    ppermute x4, starting transfers between devices, chunk_sums(): across[s] = lax.ppermute(pairs[s], 'dp', [(1, 2), (2, 1)])  14.3 us
    ppermute x4, waiting for transfers between devices, begin(): inward[c] = lax.ppermute(parts[c], 'dp', [(0, 1), (3, 2)])  12.2 us
    ppermute x3, waiting for transfers between devices, exchange_gradients(): crossed = lax.ppermute(received, 'mp', [(p, p ^ 2) for p in range(parts)])  9.6 us
    ppermute x3, starting transfers between devices, exchange_gradients(): lax.ppermute(block, 'dp', [(e, (e + k) % shards) for e in range(shards)])  5.63 us
    pallas_call x1, Pallas kernels, compact(): pl.pallas_call(functools.partial(compact_kernel, sizes), in_specs=[pl.Blo...  5.61 us
  transfers between devices with their start and end apart: 30, of which 8 were waited for; matrix products, arithmetic and copies ran while one was open for 10% of the time, Pallas kernels for 20%

commit v1 on v0

--- a/solution.py
+++ b/solution.py
@@ -265,7 +265,7 @@
         if s >= 2:
             got = after(outward[s - 2], sums.get(s - 1))
             done[s - 2] = jnp.where(middle, sums[s - 2], got)
-    return [after(done[c], sums[min(c + 3, count - 1)]) for c in range(count)]
+    return [after(done[c], sums[min(c + 2, count - 1)]) for c in range(count)]
 
 
 def rotate_and_square(

time: 155 us -> 152 us (0.981)
  waiting for transfers between devices: 36.9 us -> 32.4 us
    ppermute x4, waiting for transfers between devices: 15.1 us -> 10.6 us  [chunk_sums(): across[s] = lax.ppermute(pairs[s], 'dp', [(1, 2), (2, 1)])]
  transfers between devices with their start and end apart: 30 -> 30, of which waited for: 8 -> 7; matrix products, arithmetic and copies ran while one was open for 10% -> 10% of each run, Pallas kernels for 20% -> 21%
where the time goes in v1:
time: 152 us; the launch traced here: 150 us
  starting transfers between devices  50.1 us (33%)
  Pallas kernels  47.8 us (31%)
  waiting for transfers between devices  32.4 us (21%)
  other arithmetic  6.35 us (4%)
  matrix products  5.84 us (4%)
  local copies, waits for them, and re-layouts  5.65 us (4%)
    pallas_call x4, Pallas kernels, squares(): pl.pallas_call(functools.partial(squares_kernel, seqs, scale), grid_spec=...  26.7 us
    pallas_call x4, Pallas kernels, rotate(): pl.pallas_call(rotate_kernel, grid=(-(-size // TILE),), in_specs=[pl.Bloc...  14.5 us
    ppermute x4, starting transfers between devices, chunk_sums(): across[s] = lax.ppermute(pairs[s], 'dp', [(1, 2), (2, 1)])  14.3 us
    ppermute x4, waiting for transfers between devices, begin(): inward[c] = lax.ppermute(parts[c], 'dp', [(0, 1), (3, 2)])  12.2 us
    ppermute x4, waiting for transfers between devices, chunk_sums(): across[s] = lax.ppermute(pairs[s], 'dp', [(1, 2), (2, 1)])  10.6 us
    ppermute x3, waiting for transfers between devices, exchange_gradients(): crossed = lax.ppermute(received, 'mp', [(p, p ^ 2) for p in range(parts)])  9.6 us
    ppermute x3, starting transfers between devices, exchange_gradients(): lax.ppermute(block, 'dp', [(e, (e + k) % shards) for e in range(shards)])  5.63 us
    pallas_call x1, Pallas kernels, compact(): pl.pallas_call(functools.partial(compact_kernel, sizes), in_specs=[pl.Blo...  5.61 us
  transfers between devices with their start and end apart: 30, of which 7 were waited for; matrix products, arithmetic and copies ran while one was open for 10% of the time, Pallas kernels for 21%

profile of v1, /device:TPU:13, one launch (start us, length us, event | category | flops | bytes accessed | tf_op | source)
XLA Modules:
  0.0 149.9 jit_solution(1106472289159246247)
XLA Ops:
  0.0 1.5 %fusion.51 = (bf16[32,3200]{1,0:T(8,128)(2,1)S(1)}, bf16[32,3200]{1,0:T(8,128)(2,1)S(1)}, bf16[32,3200]{1,0:T(8,128)(2,1)S(1)}) fusion(bf16[128,12800]{1,0:T(8,128)(2,1)} %param.8, s32[]{:T(128)S(6)} %select_n.280, s32[]{:T(128)S(6)} %select_n.286, s32[]{:T(128)S(6)} %select_n.284, s32[]{:T(128)S(6)} %select_n.282), kind=kLoop, calls=%fused_computation.118 | loop fusion | bytes 1228816 | tf_op jit(solution)/shard_map/dynamic_slice | solution.py:158
  1.8 1.3 collective-permute-start.33
  3.0 4.1 %collective-permute-start.29 = (bf16[32,3200]{1,0:T(8,128)(2,1)S(1)}, bf16[32,3200]{1,0:T(8,128)(2,1)S(1)}, u32[]{:S(2)}, u32[]{:S(2)}) collective-permute-start(bf16[32,3200]{1,0:T(8,128)(2,1)S(1)} %get-tuple-element.191), channel_id=1, source_target_pairs={{0,8},{4,12},{8,0},{12,4},{1,9},{5,13},{9,1},{13,5},{2,10},{6,14},... | collective-permute-start | bytes 614408 | tf_op jit(solution)/shard_map/ppermute | solution.py:160
  8.4 4.1 %convolution_convert_fusion = bf16[128,640]{1,0:T(8,128)(2,1)S(1)} fusion(bf16[128,5120]{1,0:T(8,128)(2,1)S(1)} %copy-done, bf16[5120,640]{1,0:T(8,128)(2,1)} %param.9), kind=kOutput, calls=%fused_computation.64 | convolution fusion | flops 838942720 | bytes 8028160 | tf_op jit(solution)/shard_map/dot_general | solution.py:313
  13.1 1.2 constant_dynamic-slice_fusion
  14.5 1.8 %collective-permute-start.39 = (bf16[32,3200]{1,0:T(8,128)(2,1)S(1)}, bf16[32,3200]{1,0:T(8,128)(2,1)S(1)}, u32[]{:S(2)}, u32[]{:S(2)}) collective-permute-start(bf16[32,3200]{1,0:T(8,128)(2,1)S(1)} %collective-permute-done.37), channel_id=1, source_target_pairs={{0,1},{1,0},{2,3},{3,2},{4,5},{5,4},{6,7},{7,6},{8,9},{9,8},{10,11... | collective-permute-start | bytes 614408 | tf_op jit(solution)/shard_map/ppermute | solution.py:165
  16.3 3.9 %collective-permute-start.38 = (bf16[32,3200]{1,0:T(8,128)(2,1)S(1)}, bf16[32,3200]{1,0:T(8,128)(2,1)S(1)}, u32[]{:S(2)}, u32[]{:S(2)}) collective-permute-start(bf16[32,3200]{1,0:T(8,128)(2,1)S(1)} %collective-permute-done.37), channel_id=1, source_target_pairs={{0,2},{1,3},{2,0},{3,1},{4,6},{5,7},{6,4},{7,5},{8,10},{9,11},{10,... | collective-permute-start | bytes 614408 | tf_op jit(solution)/shard_map/ppermute | solution.py:162
  20.2 1.5 collective-permute-start.30
  21.8 1.4 collective-permute-start.35
  23.3 2.3 %collective-permute-done.38 = bf16[32,3200]{1,0:T(8,128)(2,1)S(1)} collective-permute-done((bf16[32,3200]{1,0:T(8,128)(2,1)S(1)}, bf16[32,3200]{1,0:T(8,128)(2,1)S(1)}, u32[]{:S(2)}, u32[]{:S(2)}) %collective-permute-start.38) | collective-permute-done | bytes 204832 | tf_op jit(solution)/shard_map/ppermute | solution.py:162
  26.4 3.6 %collective-permute-done.34 = bf16[32,3200]{1,0:T(8,128)(2,1)S(1)} collective-permute-done((bf16[32,3200]{1,0:T(8,128)(2,1)S(1)}, bf16[32,3200]{1,0:T(8,128)(2,1)S(1)}, u32[]{:S(2)}, u32[]{:S(2)}) %collective-permute-start.34) | collective-permute-done | bytes 204832 | tf_op jit(solution)/shard_map/ppermute | solution.py:162
  30.8 3.6 %collective-permute-done.30 = bf16[32,3200]{1,0:T(8,128)(2,1)S(1)} collective-permute-done((bf16[32,3200]{1,0:T(8,128)(2,1)S(1)}, bf16[32,3200]{1,0:T(8,128)(2,1)S(1)}, u32[]{:S(2)}, u32[]{:S(2)}) %collective-permute-start.30) | collective-permute-done | bytes 204832 | tf_op jit(solution)/shard_map/ppermute | solution.py:162
  36.4 112.3 %conditional.1 = (f32[640,3200]{1,0:T(8,128)}) conditional(s32[]{:T(128)} %bitcast.8, (s32[16]{0:T(128)S(1)}, s32[512]{0:T(512)S(1)}, bf16[128,3200]{1,0:T(8,128)(2,1)S(1)}, bf16[32,3200]{1,0:T(8,128)(2,1)S(1)}, bf16[32,3200]{1,0:T(8,128)(2,1)S(1)}, /*index=5*/bf16[32,3200]{1,0:T(8,128)(2,1)S(1)}, bf16[32,3200]{1,0:T(8,128)(2,1)S(1)}, ...), branch_computations={%region_3.4_spmd, %region_4.5_spmd} | conditional | flops 1359950592 | bytes 166810688 | solution.py:343
  36.4 5.6 %compact_rows.2.rows_ref = bf16[352,3200]{1,0:T(8,128)(2,1)S(1)} custom-call(s32[1,512]{1,0:T(1,128)S(1)} %bitcast.15, bf16[128,3200]{1,0:T(8,128)(2,1)S(1)} %get-tuple-element.87.refs_0_, bf16[32,3200]{1,0:T(8,128)(2,1)S(1)} %get-tuple-element.88.refs_1_, bf16[32,3200]{1,0:T(8,128)(2,1)S(1)} %get-tuple-element.89.refs_2_, ...), custom_call_target="tpu_custom_call" | custom-call | tf_op jit(solution)/shard_map/cond/branch_0_fun/compact_rows/pallas_call | solution.py:53
  42.0 5.0 %rotate_chunk.6 = bf16[352,768]{1,0:T(8,128)(2,1)S(1)} custom-call(bf16[352,3200]{1,0:T(8,128)(2,1)S(1)} %compact_rows.2.rows_ref, bf16[3200,3200]{1,0:T(8,128)(2,1)} %get-tuple-element.100.basis_ref), custom_call_target="tpu_custom_call" | custom-call | flops 1 | bytes 1 | tf_op jit(solution)/shard_map/cond/branch_0_fun/rotate_chunk/pallas_call | solution.py:79
  47.0 1.6 %collective-permute-start.2 = (bf16[128,640]{1,0:T(8,128)(2,1)S(1)}, bf16[128,640]{1,0:T(8,128)(2,1)S(1)}, u32[]{:S(2)}, u32[]{:S(2)}) collective-permute-start(bf16[128,640]{1,0:T(8,128)(2,1)S(1)} %get-tuple-element.101.refs_0_), channel_id=1, source_target_pairs={{12,0},{1,5},{6,10},{11,15},{28,16},{17,21},{22,26},{27,31}} | collective-permute-start | bytes 491528 | tf_op jit(solution)/shard_map/cond/branch_0_fun/ppermute | solution.py:211
  48.6 1.6 %collective-permute-start.1 = (bf16[128,640]{1,0:T(8,128)(2,1)S(1)}, bf16[128,640]{1,0:T(8,128)(2,1)S(1)}, u32[]{:S(2)}, u32[]{:S(2)}) collective-permute-start(bf16[128,640]{1,0:T(8,128)(2,1)S(1)} %get-tuple-element.101.refs_0_), channel_id=1, source_target_pairs={{8,0},{13,5},{2,10},{7,15},{24,16},{29,21},{18,26},{23,31}} | collective-permute-start | bytes 491528 | tf_op jit(solution)/shard_map/cond/branch_0_fun/ppermute | solution.py:211
  50.1 1.3 collective-permute-start
  51.4 1.3 collective-permute-start.9
  52.8 3.8 %rotate_chunk.7 = bf16[352,1024]{1,0:T(8,128)(2,1)S(1)} custom-call(bf16[352,3200]{1,0:T(8,128)(2,1)S(1)} %compact_rows.2.rows_ref, bf16[3200,3200]{1,0:T(8,128)(2,1)S(1)} %copy-done.2), custom_call_target="tpu_custom_call" | custom-call | flops 1 | bytes 1 | tf_op jit(solution)/shard_map/cond/branch_0_fun/rotate_chunk/pallas_call | solution.py:79
  56.5 1.3 collective-permute-start.6
  57.9 2.8 %rotate_chunk.8 = bf16[352,768]{1,0:T(8,128)(2,1)S(1)} custom-call(bf16[352,3200]{1,0:T(8,128)(2,1)S(1)} %compact_rows.2.rows_ref, bf16[3200,3200]{1,0:T(8,128)(2,1)S(1)} %copy-done.2), custom_call_target="tpu_custom_call" | custom-call | flops 1 | bytes 1 | tf_op jit(solution)/shard_map/cond/branch_0_fun/rotate_chunk/pallas_call | solution.py:79
  60.7 3.0 %rotate_chunk.9 = bf16[352,640]{1,0:T(8,128)(2,1)S(1)} custom-call(bf16[352,3200]{1,0:T(8,128)(2,1)S(1)} %compact_rows.2.rows_ref, bf16[3200,3200]{1,0:T(8,128)(2,1)S(1)} %copy-done.2), custom_call_target="tpu_custom_call" | custom-call | flops 1 | bytes 1 | tf_op jit(solution)/shard_map/cond/branch_0_fun/rotate_chunk/pallas_call | solution.py:79
  63.7 1.3 collective-permute-start.8
  65.0 1.3 collective-permute-start.5
  67.3 2.9 %collective-permute-start.3 = (bf16[512,640]{1,0:T(8,128)(2,1)S(1)}, bf16[512,640]{1,0:T(8,128)(2,1)}, u32[]{:S(2)}, u32[]{:S(2)}) collective-permute-start(bf16[512,640]{1,0:T(8,128)(2,1)S(1)} %stack_rows.2), channel_id=1, source_target_pairs={{0,2},{5,7},{10,8},{15,13},{16,18},{21,23},{26,24},{31,29}} | collective-permute-start | bytes 1966088 | tf_op jit(solution)/shard_map/cond/branch_0_fun/ppermute | solution.py:221
  70.3 1.2 add_convert_fusion.5
  71.5 2.6 %collective-permute-start.10 = (bf16[352,768]{1,0:T(8,128)(2,1)S(1)}, bf16[352,768]{1,0:T(8,128)(2,1)S(1)}, u32[]{:S(2)}, u32[]{:S(2)}) collective-permute-start(bf16[352,768]{1,0:T(8,128)(2,1)S(1)} %add_convert_fusion.5), channel_id=1, source_target_pairs={{4,8},{8,4},{5,9},{9,5},{6,10},{10,6},{7,11},{11,7},{20,24},{24,20... | collective-permute-start | bytes 1622024 | tf_op jit(solution)/shard_map/cond/branch_0_fun/ppermute | solution.py:260
  74.1 9.0 %collective-permute-done.6 = bf16[352,1024]{1,0:T(8,128)(2,1)} collective-permute-done((bf16[352,1024]{1,0:T(8,128)(2,1)S(1)}, bf16[352,1024]{1,0:T(8,128)(2,1)}, u32[]{:S(2)}, u32[]{:S(2)}) %collective-permute-start.6) | collective-permute-done | bytes 720928 | tf_op jit(solution)/shard_map/cond/branch_0_fun/ppermute | solution.py:253
  83.2 1.4 add_convert_fusion.1
  84.5 4.1 %collective-permute-start.7 = (bf16[352,1024]{1,0:T(8,128)(2,1)S(1)}, bf16[352,1024]{1,0:T(8,128)(2,1)S(1)}, u32[]{:S(2)}, u32[]{:S(2)}) collective-permute-start(bf16[352,1024]{1,0:T(8,128)(2,1)S(1)} %add_convert_fusion.1), channel_id=1, source_target_pairs={{4,8},{8,4},{5,9},{9,5},{6,10},{10,6},{7,11},{11,7},{20,24},{24,20... | collective-permute-start | bytes 2162696 | tf_op jit(solution)/shard_map/cond/branch_0_fun/ppermute | solution.py:260
  88.7 1.3 collective-permute-start.4
  90.2 1.3 collective-permute-start.11
  91.6 3.2 %collective-permute-done.8 = bf16[352,768]{1,0:T(8,128)(2,1)} collective-permute-done((bf16[352,768]{1,0:T(8,128)(2,1)S(1)}, bf16[352,768]{1,0:T(8,128)(2,1)}, u32[]{:S(2)}, u32[]{:S(2)}) %collective-permute-start.8) | collective-permute-done | bytes 540704 | tf_op jit(solution)/shard_map/cond/branch_0_fun/ppermute | solution.py:253
  94.7 1.2 add_convert_fusion.3
  95.9 4.1 %collective-permute-start.14 = (bf16[352,768]{1,0:T(8,128)(2,1)S(1)}, bf16[352,768]{1,0:T(8,128)(2,1)S(1)}, u32[]{:S(2)}, u32[]{:S(2)}) collective-permute-start(bf16[352,768]{1,0:T(8,128)(2,1)S(1)} %add_convert_fusion.3), channel_id=1, source_target_pairs={{4,8},{8,4},{5,9},{9,5},{6,10},{10,6},{7,11},{11,7},{20,24},{24,20... | collective-permute-start | bytes 1622024 | tf_op jit(solution)/shard_map/cond/branch_0_fun/ppermute | solution.py:260
  100.0 5.4 %collective-permute-done.7 = bf16[352,1024]{1,0:T(8,128)(2,1)S(1)} collective-permute-done((bf16[352,1024]{1,0:T(8,128)(2,1)S(1)}, bf16[352,1024]{1,0:T(8,128)(2,1)S(1)}, u32[]{:S(2)}, u32[]{:S(2)}) %collective-permute-start.7) | collective-permute-done | bytes 720928 | tf_op jit(solution)/shard_map/cond/branch_0_fun/ppermute | solution.py:260
  105.6 1.3 collective-permute-start.16
  108.2 3.5 %collective-permute-start.12 = (bf16[352,640]{1,0:T(8,128)(2,1)S(1)}, bf16[352,640]{1,0:T(8,128)(2,1)S(1)}, u32[]{:S(2)}, u32[]{:S(2)}) collective-permute-start(bf16[352,640]{1,0:T(8,128)(2,1)S(1)} %add_convert_fusion.7), channel_id=1, source_target_pairs={{4,8},{8,4},{5,9},{9,5},{6,10},{10,6},{7,11},{11,7},{20,24},{24,20... | collective-permute-start | bytes 1351688 | tf_op jit(solution)/shard_map/cond/branch_0_fun/ppermute | solution.py:260
  111.8 5.2 %collective-permute-done.14 = bf16[352,768]{1,0:T(8,128)(2,1)S(1)} collective-permute-done((bf16[352,768]{1,0:T(8,128)(2,1)S(1)}, bf16[352,768]{1,0:T(8,128)(2,1)S(1)}, u32[]{:S(2)}, u32[]{:S(2)}) %collective-permute-start.14) | collective-permute-done | bytes 540704 | tf_op jit(solution)/shard_map/cond/branch_0_fun/ppermute | solution.py:260
  117.1 1.3 collective-permute-start.15
  118.4 1.8 %fusion.2.at_ref = bf16[640,2048]{1,0:T(8,128)(2,1)S(1)} fusion(s32[2048]{0:T(1024)S(1)} %select_bitcast_fusion, s32[512]{0:T(512)S(1)} %add_bitcast_fusion, bf16[512,640]{1,0:T(8,128)(2,1)S(1)} %broadcast_select_fusion.1, bf16[512,640]{1,0:T(8,128)(2,1)S(1)} %collective-permute-done.4, pred[]{:T(512)S(6)} %or.8), kind=kOutput, calls=%fused_computation.2 | convolution fusion | flops 1344864256 | bytes 3942401 | tf_op jit(solution)/shard_map/cond/branch_0_fun/dot_general | solution.py:294
  120.2 6.3 %sum_squares.6.refs_0_ = f32[640,3200]{1,0:T(8,128)} custom-call(s32[16]{0:T(128)S(1)} %multiply_minimum_fusion.window_starts, bf16[640,2048]{1,0:T(8,128)(2,1)S(1)} %fusion.2.at_ref, bf16[352,768]{1,0:T(8,128)(2,1)S(1)} %broadcast_select_fusion.3.gt_ref), custom_call_target="tpu_custom_call" | custom-call | flops 1 | bytes 1 | tf_op jit(solution)/shard_map/cond/branch_0_fun/sum_squares/pallas_call | solution.py:129
  126.6 1.3 collective-permute-start.13
  128.0 7.9 %sum_squares.7.refs_0_ = f32[640,3200]{1,0:T(8,128)} custom-call(s32[16]{0:T(128)S(1)} %multiply_minimum_fusion.window_starts, bf16[640,2048]{1,0:T(8,128)(2,1)S(1)} %fusion.2.at_ref, bf16[352,1024]{1,0:T(8,128)(2,1)S(1)} %broadcast_select_fusion.gt_ref, f32[640,3200]{1,0:T(8,128)} %sum_squares.6.refs_0_), custom_call_target="tpu_custom_call", output_to_operand_aliasing={{}: (3, {})} | custom-call | flops 1 | bytes 1 | tf_op jit(solution)/shard_map/cond/branch_0_fun/sum_squares/pallas_call | solution.py:129
  136.0 6.3 %sum_squares.8.refs_0_ = f32[640,3200]{1,0:T(8,128)} custom-call(s32[16]{0:T(128)S(1)} %multiply_minimum_fusion.window_starts, bf16[640,2048]{1,0:T(8,128)(2,1)S(1)} %fusion.2.at_ref, bf16[352,768]{1,0:T(8,128)(2,1)S(1)} %broadcast_select_fusion.2.gt_ref, f32[640,3200]{1,0:T(8,128)} %sum_squares.7.refs_0_), custom_call_target="tpu_custom_call", output_to_operand_aliasing={{}: (3, {})} | custom-call | flops 1 | bytes 1 | tf_op jit(solution)/shard_map/cond/branch_0_fun/sum_squares/pallas_call | solution.py:129
  142.4 6.2 %sum_squares.9 = f32[640,3200]{1,0:T(8,128)} custom-call(s32[16]{0:T(128)S(1)} %multiply_minimum_fusion.window_starts, bf16[640,2048]{1,0:T(8,128)(2,1)S(1)} %fusion.2.at_ref, bf16[352,640]{1,0:T(8,128)(2,1)S(1)} %broadcast_select_fusion.4.gt_ref, f32[640,3200]{1,0:T(8,128)} %sum_squares.8.refs_0_), custom_call_target="tpu_custom_call", output_to_operand_aliasing={{}: (3, {})} | custom-call | flops 1 | bytes 1 | tf_op jit(solution)/shard_map/cond/branch_0_fun/sum_squares/pallas_call | solution.py:129
  148.6 1.3 copy-done.1
  (67 shorter events, 8.0 us)
Async XLA Ops:
  0.0 8.4 %copy-start = (bf16[128,5120]{1,0:T(8,128)(2,1)S(1)}, bf16[128,5120]{1,0:T(8,128)(2,1)}, u32[]{:S(2)}) copy-start(bf16[128,5120]{1,0:T(8,128)(2,1)} %param.7) | copy-start | bytes 3932164
  1.5 13.0 %collective-permute-start.37 = (bf16[32,3200]{1,0:T(8,128)(2,1)S(1)}, bf16[32,3200]{1,0:T(8,128)(2,1)S(1)}, u32[]{:S(2)}, u32[]{:S(2)}) collective-permute-start(bf16[32,3200]{1,0:T(8,128)(2,1)S(1)} %get-tuple-element.189), channel_id=1, source_target_pairs={{0,12},{4,0},{8,4},{12,8},{1,13},{5,1},{9,5},{13,9},{2,14},{6,2},{... | collective-permute-start | bytes 614408 | tf_op jit(solution)/shard_map/ppermute | solution.py:160
  1.8 18.4 %collective-permute-start.33 = (bf16[32,3200]{1,0:T(8,128)(2,1)S(1)}, bf16[32,3200]{1,0:T(8,128)(2,1)S(1)}, u32[]{:S(2)}, u32[]{:S(2)}) collective-permute-start(bf16[32,3200]{1,0:T(8,128)(2,1)S(1)} %get-tuple-element.190), channel_id=1, source_target_pairs={{0,4},{4,8},{8,12},{12,0},{1,5},{5,9},{9,13},{13,1},{2,6},{6,10},{... | collective-permute-start | bytes 614408 | tf_op jit(solution)/shard_map/ppermute | solution.py:160
  3.0 17.2 %collective-permute-start.29 = (bf16[32,3200]{1,0:T(8,128)(2,1)S(1)}, bf16[32,3200]{1,0:T(8,128)(2,1)S(1)}, u32[]{:S(2)}, u32[]{:S(2)}) collective-permute-start(bf16[32,3200]{1,0:T(8,128)(2,1)S(1)} %get-tuple-element.191), channel_id=1, source_target_pairs={{0,8},{4,12},{8,0},{12,4},{1,9},{5,13},{9,1},{13,5},{2,10},{6,14},... | collective-permute-start | bytes 614408 | tf_op jit(solution)/shard_map/ppermute | solution.py:160
  8.4 4.5 %copy-start.9 = (s32[16]{0:T(128)S(1)}, s32[16]{0:T(128)}, u32[]{:S(2)}) copy-start(s32[16]{0:T(128)} %param.11) | copy-start | bytes 196
  12.5 9.3 %collective-permute-start.28 = (s32[1]{0:T(128)}, s32[1]{0:T(128)}, u32[]{:S(2)}, u32[]{:S(2)}) collective-permute-start(s32[1]{0:T(128)} %bitcast.7), channel_id=1, source_target_pairs={{0,16},{16,0},{1,17},{17,1},{2,18},{18,2},{3,19},{19,3},{4,20},{20... | collective-permute-start | bytes 20 | tf_op jit(solution)/shard_map/ppermute | solution.py:337
  14.5 8.7 %collective-permute-start.39 = (bf16[32,3200]{1,0:T(8,128)(2,1)S(1)}, bf16[32,3200]{1,0:T(8,128)(2,1)S(1)}, u32[]{:S(2)}, u32[]{:S(2)}) collective-permute-start(bf16[32,3200]{1,0:T(8,128)(2,1)S(1)} %collective-permute-done.37), channel_id=1, source_target_pairs={{0,1},{1,0},{2,3},{3,2},{4,5},{5,4},{6,7},{7,6},{8,9},{9,8},{10,11... | collective-permute-start | bytes 614408 | tf_op jit(solution)/shard_map/ppermute | solution.py:165
  16.3 9.3 %collective-permute-start.38 = (bf16[32,3200]{1,0:T(8,128)(2,1)S(1)}, bf16[32,3200]{1,0:T(8,128)(2,1)S(1)}, u32[]{:S(2)}, u32[]{:S(2)}) collective-permute-start(bf16[32,3200]{1,0:T(8,128)(2,1)S(1)} %collective-permute-done.37), channel_id=1, source_target_pairs={{0,2},{1,3},{2,0},{3,1},{4,6},{5,7},{6,4},{7,5},{8,10},{9,11},{10,... | collective-permute-start | bytes 614408 | tf_op jit(solution)/shard_map/ppermute | solution.py:162
  20.2 9.8 %collective-permute-start.34 = (bf16[32,3200]{1,0:T(8,128)(2,1)S(1)}, bf16[32,3200]{1,0:T(8,128)(2,1)S(1)}, u32[]{:S(2)}, u32[]{:S(2)}) collective-permute-start(bf16[32,3200]{1,0:T(8,128)(2,1)S(1)} %collective-permute-done.33), channel_id=1, source_target_pairs={{0,2},{1,3},{2,0},{3,1},{4,6},{5,7},{6,4},{7,5},{8,10},{9,11},{10,... | collective-permute-start | bytes 614408 | tf_op jit(solution)/shard_map/ppermute | solution.py:162
  20.2 14.2 %collective-permute-start.30 = (bf16[32,3200]{1,0:T(8,128)(2,1)S(1)}, bf16[32,3200]{1,0:T(8,128)(2,1)S(1)}, u32[]{:S(2)}, u32[]{:S(2)}) collective-permute-start(bf16[32,3200]{1,0:T(8,128)(2,1)S(1)} %collective-permute-done.29), channel_id=1, source_target_pairs={{0,2},{1,3},{2,0},{3,1},{4,6},{5,7},{6,4},{7,5},{8,10},{9,11},{10,... | collective-permute-start | bytes 614408 | tf_op jit(solution)/shard_map/ppermute | solution.py:162
  21.8 14.5 %collective-permute-start.35 = (bf16[32,3200]{1,0:T(8,128)(2,1)S(1)}, bf16[32,3200]{1,0:T(8,128)(2,1)S(1)}, u32[]{:S(2)}, u32[]{:S(2)}) collective-permute-start(bf16[32,3200]{1,0:T(8,128)(2,1)S(1)} %collective-permute-done.33), channel_id=1, source_target_pairs={{0,1},{1,0},{2,3},{3,2},{4,5},{5,4},{6,7},{7,6},{8,9},{9,8},{10,11... | collective-permute-start | bytes 614408 | tf_op jit(solution)/shard_map/ppermute | solution.py:165
  23.2 13.1 %collective-permute-start.31 = (bf16[32,3200]{1,0:T(8,128)(2,1)S(1)}, bf16[32,3200]{1,0:T(8,128)(2,1)S(1)}, u32[]{:S(2)}, u32[]{:S(2)}) collective-permute-start(bf16[32,3200]{1,0:T(8,128)(2,1)S(1)} %collective-permute-done.29), channel_id=1, source_target_pairs={{0,1},{1,0},{2,3},{3,2},{4,5},{5,4},{6,7},{7,6},{8,9},{9,8},{10,11... | collective-permute-start | bytes 614408 | tf_op jit(solution)/shard_map/ppermute | solution.py:165
  25.6 10.7 %collective-permute-start.40 = (bf16[32,3200]{1,0:T(8,128)(2,1)S(1)}, bf16[32,3200]{1,0:T(8,128)(2,1)}, u32[]{:S(2)}, u32[]{:S(2)}) collective-permute-start(bf16[32,3200]{1,0:T(8,128)(2,1)S(1)} %collective-permute-done.38), channel_id=1, source_target_pairs={{0,1},{1,0},{2,3},{3,2},{4,5},{5,4},{6,7},{7,6},{8,9},{9,8},{10,11... | collective-permute-start | bytes 614408 | tf_op jit(solution)/shard_map/ppermute | solution.py:165
  30.0 6.3 %collective-permute-start.36 = (bf16[32,3200]{1,0:T(8,128)(2,1)S(1)}, bf16[32,3200]{1,0:T(8,128)(2,1)S(1)}, u32[]{:S(2)}, u32[]{:S(2)}) collective-permute-start(bf16[32,3200]{1,0:T(8,128)(2,1)S(1)} %collective-permute-done.34), channel_id=1, source_target_pairs={{0,1},{1,0},{2,3},{3,2},{4,5},{5,4},{6,7},{7,6},{8,9},{9,8},{10,11... | collective-permute-start | bytes 614408 | tf_op jit(solution)/shard_map/ppermute | solution.py:165
  34.4 1.9 %collective-permute-start.32 = (bf16[32,3200]{1,0:T(8,128)(2,1)S(1)}, bf16[32,3200]{1,0:T(8,128)(2,1)S(1)}, u32[]{:S(2)}, u32[]{:S(2)}) collective-permute-start(bf16[32,3200]{1,0:T(8,128)(2,1)S(1)} %collective-permute-done.30), channel_id=1, source_target_pairs={{0,1},{1,0},{2,3},{3,2},{4,5},{5,4},{6,7},{7,6},{8,9},{9,8},{10,11... | collective-permute-start | bytes 614408 | tf_op jit(solution)/shard_map/ppermute | solution.py:165
  36.4 13.8 %copy-start.4 = (bf16[128,640]{1,0:T(8,128)(2,1)}, bf16[128,640]{1,0:T(8,128)(2,1)S(1)}, u32[]{:S(2)}) copy-start(bf16[128,640]{1,0:T(8,128)(2,1)S(1)} %get-tuple-element.101.refs_0_) | copy-start | bytes 491524 | tf_op jit(solution)/shard_map/cond
  42.0 10.7 %copy-start.2 = (bf16[3200,3200]{1,0:T(8,128)(2,1)S(1)}, bf16[3200,3200]{1,0:T(8,128)(2,1)}, u32[]{:S(2)}) copy-start(bf16[3200,3200]{1,0:T(8,128)(2,1)} %get-tuple-element.100.basis_ref) | copy-start | bytes 61440004 | tf_op jit(solution)/shard_map/cond
  47.0 16.7 %collective-permute-start.2 = (bf16[128,640]{1,0:T(8,128)(2,1)S(1)}, bf16[128,640]{1,0:T(8,128)(2,1)S(1)}, u32[]{:S(2)}, u32[]{:S(2)}) collective-permute-start(bf16[128,640]{1,0:T(8,128)(2,1)S(1)} %get-tuple-element.101.refs_0_), channel_id=1, source_target_pairs={{12,0},{1,5},{6,10},{11,15},{28,16},{17,21},{22,26},{27,31}} | collective-permute-start | bytes 491528 | tf_op jit(solution)/shard_map/cond/branch_0_fun/ppermute | solution.py:211
  48.6 16.5 %collective-permute-start.1 = (bf16[128,640]{1,0:T(8,128)(2,1)S(1)}, bf16[128,640]{1,0:T(8,128)(2,1)S(1)}, u32[]{:S(2)}, u32[]{:S(2)}) collective-permute-start(bf16[128,640]{1,0:T(8,128)(2,1)S(1)} %get-tuple-element.101.refs_0_), channel_id=1, source_target_pairs={{8,0},{13,5},{2,10},{7,15},{24,16},{29,21},{18,26},{23,31}} | collective-permute-start | bytes 491528 | tf_op jit(solution)/shard_map/cond/branch_0_fun/ppermute | solution.py:211
  50.1 16.2 %collective-permute-start = (bf16[128,640]{1,0:T(8,128)(2,1)S(1)}, bf16[128,640]{1,0:T(8,128)(2,1)S(1)}, u32[]{:S(2)}, u32[]{:S(2)}) collective-permute-start(bf16[128,640]{1,0:T(8,128)(2,1)S(1)} %get-tuple-element.101.refs_0_), channel_id=1, source_target_pairs={{4,0},{9,5},{14,10},{3,15},{20,16},{25,21},{30,26},{19,31}} | collective-permute-start | bytes 491528 | tf_op jit(solution)/shard_map/cond/branch_0_fun/ppermute | solution.py:211
  51.4 18.9 %collective-permute-start.9 = (bf16[352,768]{1,0:T(8,128)(2,1)S(1)}, bf16[352,768]{1,0:T(8,128)(2,1)}, u32[]{:S(2)}, u32[]{:S(2)}) collective-permute-start(bf16[352,768]{1,0:T(8,128)(2,1)S(1)} %rotate_chunk.6), channel_id=1, source_target_pairs={{0,4},{12,8},{1,5},{13,9},{2,6},{14,10},{3,7},{15,11},{16,20},{28,... | collective-permute-start | bytes 1622024 | tf_op jit(solution)/shard_map/cond/branch_0_fun/ppermute | solution.py:253
  56.5 26.6 %collective-permute-start.6 = (bf16[352,1024]{1,0:T(8,128)(2,1)S(1)}, bf16[352,1024]{1,0:T(8,128)(2,1)}, u32[]{:S(2)}, u32[]{:S(2)}) collective-permute-start(bf16[352,1024]{1,0:T(8,128)(2,1)S(1)} %rotate_chunk.7), channel_id=1, source_target_pairs={{0,4},{12,8},{1,5},{13,9},{2,6},{14,10},{3,7},{15,11},{16,20},{28,... | collective-permute-start | bytes 2162696 | tf_op jit(solution)/shard_map/cond/branch_0_fun/ppermute | solution.py:253
  63.7 31.0 %collective-permute-start.8 = (bf16[352,768]{1,0:T(8,128)(2,1)S(1)}, bf16[352,768]{1,0:T(8,128)(2,1)}, u32[]{:S(2)}, u32[]{:S(2)}) collective-permute-start(bf16[352,768]{1,0:T(8,128)(2,1)S(1)} %rotate_chunk.8), channel_id=1, source_target_pairs={{0,4},{12,8},{1,5},{13,9},{2,6},{14,10},{3,7},{15,11},{16,20},{28,... | collective-permute-start | bytes 1622024 | tf_op jit(solution)/shard_map/cond/branch_0_fun/ppermute | solution.py:253
  65.0 42.0 %collective-permute-start.5 = (bf16[352,640]{1,0:T(8,128)(2,1)S(1)}, bf16[352,640]{1,0:T(8,128)(2,1)}, u32[]{:S(2)}, u32[]{:S(2)}) collective-permute-start(bf16[352,640]{1,0:T(8,128)(2,1)S(1)} %rotate_chunk.9), channel_id=1, source_target_pairs={{0,4},{12,8},{1,5},{13,9},{2,6},{14,10},{3,7},{15,11},{16,20},{28,... | collective-permute-start | bytes 1351688 | tf_op jit(solution)/shard_map/cond/branch_0_fun/ppermute | solution.py:253
  67.3 21.3 %collective-permute-start.3 = (bf16[512,640]{1,0:T(8,128)(2,1)S(1)}, bf16[512,640]{1,0:T(8,128)(2,1)}, u32[]{:S(2)}, u32[]{:S(2)}) collective-permute-start(bf16[512,640]{1,0:T(8,128)(2,1)S(1)} %stack_rows.2), channel_id=1, source_target_pairs={{0,2},{5,7},{10,8},{15,13},{16,18},{21,23},{26,24},{31,29}} | collective-permute-start | bytes 1966088 | tf_op jit(solution)/shard_map/cond/branch_0_fun/ppermute | solution.py:221
  71.5 18.6 %collective-permute-start.10 = (bf16[352,768]{1,0:T(8,128)(2,1)S(1)}, bf16[352,768]{1,0:T(8,128)(2,1)S(1)}, u32[]{:S(2)}, u32[]{:S(2)}) collective-permute-start(bf16[352,768]{1,0:T(8,128)(2,1)S(1)} %add_convert_fusion.5), channel_id=1, source_target_pairs={{4,8},{8,4},{5,9},{9,5},{6,10},{10,6},{7,11},{11,7},{20,24},{24,20... | collective-permute-start | bytes 1622024 | tf_op jit(solution)/shard_map/cond/branch_0_fun/ppermute | solution.py:260
  84.5 20.8 %collective-permute-start.7 = (bf16[352,1024]{1,0:T(8,128)(2,1)S(1)}, bf16[352,1024]{1,0:T(8,128)(2,1)S(1)}, u32[]{:S(2)}, u32[]{:S(2)}) collective-permute-start(bf16[352,1024]{1,0:T(8,128)(2,1)S(1)} %add_convert_fusion.1), channel_id=1, source_target_pairs={{4,8},{8,4},{5,9},{9,5},{6,10},{10,6},{7,11},{11,7},{20,24},{24,20... | collective-permute-start | bytes 2162696 | tf_op jit(solution)/shard_map/cond/branch_0_fun/ppermute | solution.py:260
  88.7 29.7 %collective-permute-start.4 = (bf16[512,640]{1,0:T(8,128)(2,1)S(1)}, bf16[512,640]{1,0:T(8,128)(2,1)S(1)}, u32[]{:S(2)}, u32[]{:S(2)}) collective-permute-start(bf16[512,640]{1,0:T(8,128)(2,1)S(1)} %broadcast_select_fusion.1), channel_id=1, source_target_pairs={{0,1},{2,3},{5,4},{7,6},{10,11},{8,9},{15,14},{13,12},{16,17},{18,... | collective-permute-start | bytes 1966088 | tf_op jit(solution)/shard_map/cond/branch_0_fun/ppermute | solution.py:223
  90.2 16.7 %collective-permute-start.11 = (bf16[352,768]{1,0:T(8,128)(2,1)S(1)}, bf16[352,768]{1,0:T(8,128)(2,1)S(1)}, u32[]{:S(2)}, u32[]{:S(2)}) collective-permute-start(bf16[352,768]{1,0:T(8,128)(2,1)S(1)} %add_convert_fusion.4), channel_id=1, source_target_pairs={{4,0},{8,12},{5,1},{9,13},{6,2},{10,14},{7,3},{11,15},{20,16},{24,... | collective-permute-start | bytes 1622024 | tf_op jit(solution)/shard_map/cond/branch_0_fun/ppermute | solution.py:263
  95.9 21.0 %collective-permute-start.14 = (bf16[352,768]{1,0:T(8,128)(2,1)S(1)}, bf16[352,768]{1,0:T(8,128)(2,1)S(1)}, u32[]{:S(2)}, u32[]{:S(2)}) collective-permute-start(bf16[352,768]{1,0:T(8,128)(2,1)S(1)} %add_convert_fusion.3), channel_id=1, source_target_pairs={{4,8},{8,4},{5,9},{9,5},{6,10},{10,6},{7,11},{11,7},{20,24},{24,20... | collective-permute-start | bytes 1622024 | tf_op jit(solution)/shard_map/cond/branch_0_fun/ppermute | solution.py:260
  105.6 22.3 %collective-permute-start.16 = (bf16[352,1024]{1,0:T(8,128)(2,1)S(1)}, bf16[352,1024]{1,0:T(8,128)(2,1)S(1)}, u32[]{:S(2)}, u32[]{:S(2)}) collective-permute-start(bf16[352,1024]{1,0:T(8,128)(2,1)S(1)} %add_convert_fusion), channel_id=1, source_target_pairs={{4,0},{8,12},{5,1},{9,13},{6,2},{10,14},{7,3},{11,15},{20,16},{24,... | collective-permute-start | bytes 2162696 | tf_op jit(solution)/shard_map/cond/branch_0_fun/ppermute | solution.py:263
  108.2 18.3 %collective-permute-start.12 = (bf16[352,640]{1,0:T(8,128)(2,1)S(1)}, bf16[352,640]{1,0:T(8,128)(2,1)S(1)}, u32[]{:S(2)}, u32[]{:S(2)}) collective-permute-start(bf16[352,640]{1,0:T(8,128)(2,1)S(1)} %add_convert_fusion.7), channel_id=1, source_target_pairs={{4,8},{8,4},{5,9},{9,5},{6,10},{10,6},{7,11},{11,7},{20,24},{24,20... | collective-permute-start | bytes 1351688 | tf_op jit(solution)/shard_map/cond/branch_0_fun/ppermute | solution.py:260
  117.1 18.9 %collective-permute-start.15 = (bf16[352,768]{1,0:T(8,128)(2,1)S(1)}, bf16[352,768]{1,0:T(8,128)(2,1)S(1)}, u32[]{:S(2)}, u32[]{:S(2)}) collective-permute-start(bf16[352,768]{1,0:T(8,128)(2,1)S(1)} %add_convert_fusion.2), channel_id=1, source_target_pairs={{4,0},{8,12},{5,1},{9,13},{6,2},{10,14},{7,3},{11,15},{20,16},{24,... | collective-permute-start | bytes 1622024 | tf_op jit(solution)/shard_map/cond/branch_0_fun/ppermute | solution.py:263
  126.6 15.7 %collective-permute-start.13 = (bf16[352,640]{1,0:T(8,128)(2,1)S(1)}, bf16[352,640]{1,0:T(8,128)(2,1)S(1)}, u32[]{:S(2)}, u32[]{:S(2)}) collective-permute-start(bf16[352,640]{1,0:T(8,128)(2,1)S(1)} %add_convert_fusion.6), channel_id=1, source_target_pairs={{4,0},{8,12},{5,1},{9,13},{6,2},{10,14},{7,3},{11,15},{20,16},{24,... | collective-permute-start | bytes 1351688 | tf_op jit(solution)/shard_map/cond/branch_0_fun/ppermute | solution.py:263
  148.6 1.3 copy-start.1
